TPU v7x, 32 devices: a whole 2x2x4 slice. The times are simulated.
32 devices in a mesh: rep: 4 (over y, x), fsdp: 8 (over z, core).
Axes of the slice: x: 2, y: 2, z: 4, core: 2. Of those that a mesh axis runs over, the one named last changes fastest.
Arguments:
- tokens: bfloat16 [65536, 768], P(('rep', 'fsdp')), may hold values from -6 to 6
- segment_ids: int32 [64, 1024], P(('rep', 'fsdp')), may hold values from 0 to 5, as said below
- valid_mask: int32 [64, 1024], P(('rep', 'fsdp')), may hold values from 0 to 1, as said below
- cotangent: bfloat16 [65536, 768], P(('rep', 'fsdp')), may hold values from -6 to 6
- norm1_gain: bfloat16 [768], P('fsdp'), may hold values from 0.099609375 to 1.8984375
- norm1_bias: bfloat16 [768], P('fsdp'), may hold values from -1.5 to 1.5
- qkv_weight: bfloat16 [768, 2304], P('fsdp'), may hold values from -0.21875 to 0.21875
- query_bias: bfloat16 [768], P('fsdp'), may hold values from -1.5 to 1.5
- value_bias: bfloat16 [768], P('fsdp'), may hold values from -1.5 to 1.5
- proj_weight: bfloat16 [768, 768], P('fsdp'), may hold values from -1.75 to 1.75
- proj_bias: bfloat16 [768], P('fsdp'), may hold values from -1.5 to 1.5
- norm2_gain: bfloat16 [768], P('fsdp'), may hold values from 0.099609375 to 1.8984375
- norm2_bias: bfloat16 [768], P('fsdp'), may hold values from -1.5 to 1.5
- expand_weight: bfloat16 [768, 3072], P('fsdp'), may hold values from -0.21875 to 0.21875
- expand_bias: bfloat16 [3072], P('fsdp'), may hold values from -1.5 to 1.5
- reduce_weight: bfloat16 [3072, 768], P('fsdp'), may hold values from -0.109375 to 0.109375
- reduce_bias: bfloat16 [768], P('fsdp'), may hold values from -1.5 to 1.5
Outputs:
- output: bfloat16 [65536, 768], P(('rep', 'fsdp'))
- input_grad: bfloat16 [65536, 768], P(('rep', 'fsdp'))
- grad_norm1_gain: float32 [768], P('fsdp')
- grad_norm1_bias: float32 [768], P('fsdp')
- grad_qkv_weight: float32 [768, 2304], P('fsdp')
- grad_query_bias: float32 [768], P('fsdp')
- grad_value_bias: float32 [768], P('fsdp')
- grad_proj_weight: float32 [768, 768], P('fsdp')
- grad_proj_bias: float32 [768], P('fsdp')
- grad_norm2_gain: float32 [768], P('fsdp')
- grad_norm2_bias: float32 [768], P('fsdp')
- grad_expand_weight: float32 [768, 3072], P('fsdp')
- grad_expand_bias: float32 [3072], P('fsdp')
- grad_reduce_weight: float32 [3072, 768], P('fsdp')
- grad_reduce_bias: float32 [768], P('fsdp')
Inputs may be any that keep to these rules, and one draw needn't show every extreme that they name: `segment_ids`: clip number of each row; along a sequence it never falls, each of the 6 clips holds one contiguous run of rows, and every clip of every sequence is present. `valid_mask`: inside each clip's rows the valid rows come first and padding rows follow; every clip has valid rows, and the last clip of every sequence ends in padding.
All inputs are finite; a program needn't handle non-finite values.
Results may differ from a plain program's by a relative error of at most 0.019.
Values may be sent and summed in bfloat16 or wider, within the bound.
No kernel may reach another device: no remote copies, remote signals or barrier semaphores. Data moves between devices by JAX's collectives and lax.ppermute only.
A program may use at most 448 MiB of HBM per device.

v0:
```python
from functools import partial

import jax
import jax.numpy as jnp
from jax import lax
from jax.sharding import PartitionSpec as P

HEADS = 12


epsilon = 1e-06


def layer_norm(inputs, norm_gain, norm_shift):
    row_mean = jnp.mean(inputs, axis=-1, keepdims=True)
    centred = inputs - row_mean
    row_var = jnp.mean(centred * centred, axis=-1, keepdims=True)
    return centred * lax.rsqrt(row_var + epsilon) * norm_gain + norm_shift


def block_scores(query_rows, key_heads, row_segments, segments, validity):
    score_scale = query_rows.shape[2] ** (-0.5)
    scores = (
        jnp.einsum("qhd,khd->hqk", query_rows, key_heads, preferred_element_type=jnp.float32)
        * score_scale
    )
    allowed = (row_segments[:, None] == segments[None, :]) & (validity[None, :] == 1)
    return (jnp.where(allowed[None], scores, -1e30), allowed)


def attend_sequence(packed):
    query_heads, key_heads, value_heads, segments, validity = packed
    seq_len = query_heads.shape[0]
    block_rows = min(512, seq_len)
    mixed_parts = []
    logsum_parts = []
    for offset in range(0, seq_len, block_rows):
        masked, allowed = block_scores(
            query_heads[offset : offset + block_rows],
            key_heads,
            segments[offset : offset + block_rows],
            segments,
            validity,
        )
        highest = jnp.max(masked, axis=-1, keepdims=True)
        exponent = jnp.where(allowed[None], jnp.exp(masked - highest), 0.0)
        totals = jnp.sum(exponent, axis=-1, keepdims=True)
        attn_weights = (exponent / totals).astype(jnp.bfloat16)
        mixed_parts.append(
            jnp.einsum(
                "hqk,khd->qhd", attn_weights, value_heads, preferred_element_type=jnp.float32
            ).astype(jnp.bfloat16)
        )
        logsum_parts.append(highest + jnp.log(totals))
    return (jnp.concatenate(mixed_parts, axis=0), jnp.concatenate(logsum_parts, axis=1))


def attend_back(packed):
    query_heads, key_heads, value_heads, segments, validity, logsums, grad_mixed = packed
    seq_len = query_heads.shape[0]
    score_scale = query_heads.shape[2] ** (-0.5)
    block_rows = min(512, seq_len)
    grad_keys = jnp.zeros(key_heads.shape, jnp.float32)
    grad_values = jnp.zeros(value_heads.shape, jnp.float32)
    query_parts = []
    for offset in range(0, seq_len, block_rows):
        query_rows = query_heads[offset : offset + block_rows]
        grad_rows = grad_mixed[offset : offset + block_rows]
        masked, allowed = block_scores(
            query_rows, key_heads, segments[offset : offset + block_rows], segments, validity
        )
        probs = jnp.where(
            allowed[None], jnp.exp(masked - logsums[:, offset : offset + block_rows]), 0.0
        )
        grad_probs = jnp.einsum(
            "qhd,khd->hqk", grad_rows, value_heads, preferred_element_type=jnp.float32
        )
        inner = jnp.sum(probs * grad_probs, axis=-1, keepdims=True)
        grad_scores = (probs * (grad_probs - inner)).astype(jnp.bfloat16)
        query_parts.append(
            (
                jnp.einsum(
                    "hqk,khd->qhd", grad_scores, key_heads, preferred_element_type=jnp.float32
                )
                * score_scale
            ).astype(jnp.bfloat16)
        )
        grad_keys = (
            grad_keys
            + jnp.einsum(
                "hqk,qhd->khd", grad_scores, query_rows, preferred_element_type=jnp.float32
            )
            * score_scale
        )
        grad_values = grad_values + jnp.einsum(
            "hqk,qhd->khd",
            probs.astype(jnp.bfloat16),
            grad_rows,
            preferred_element_type=jnp.float32,
        )
    return (
        jnp.concatenate(query_parts, axis=0),
        grad_keys.astype(jnp.bfloat16),
        grad_values.astype(jnp.bfloat16),
    )


def local(
    tokens,
    segment_ids,
    valid_mask,
    cotangent,
    norm1_gain,
    norm1_bias,
    qkv_weight,
    query_bias,
    value_bias,
    proj_weight,
    proj_bias,
    norm2_gain,
    norm2_bias,
    expand_weight,
    expand_bias,
    reduce_weight,
    reduce_bias,
):
    gathered = (
        lax.all_gather(norm1_gain, "fsdp", axis=0, tiled=True),
        lax.all_gather(norm1_bias, "fsdp", axis=0, tiled=True),
        lax.all_gather(qkv_weight, "fsdp", axis=0, tiled=True),
        lax.all_gather(query_bias, "fsdp", axis=0, tiled=True),
        lax.all_gather(value_bias, "fsdp", axis=0, tiled=True),
        lax.all_gather(proj_weight, "fsdp", axis=0, tiled=True),
        lax.all_gather(proj_bias, "fsdp", axis=0, tiled=True),
        lax.all_gather(norm2_gain, "fsdp", axis=0, tiled=True),
        lax.all_gather(norm2_bias, "fsdp", axis=0, tiled=True),
        lax.all_gather(expand_weight, "fsdp", axis=0, tiled=True),
        lax.all_gather(expand_bias, "fsdp", axis=0, tiled=True),
        lax.all_gather(reduce_weight, "fsdp", axis=0, tiled=True),
        lax.all_gather(reduce_bias, "fsdp", axis=0, tiled=True),
    )
    (
        full_gain1,
        full_bias1,
        full_qkv,
        full_qbias,
        full_vbias,
        full_proj,
        full_pbias,
        full_gain2,
        full_bias2,
        full_expand,
        full_ebias,
        full_reduce,
        full_rbias,
    ) = gathered
    row_count, model_width = tokens.shape
    seq_count, seq_len = segment_ids.shape
    head_size = model_width // HEADS

    def split_heads(matrix):
        return matrix.reshape(seq_count, seq_len, HEADS, head_size)

    inputs = tokens.astype(jnp.float32)
    normed1 = layer_norm(
        inputs, full_gain1.astype(jnp.float32), full_bias1.astype(jnp.float32)
    ).astype(jnp.bfloat16)
    projected = jnp.dot(normed1, full_qkv, preferred_element_type=jnp.float32)
    queries = (projected[:, :model_width] + full_qbias.astype(jnp.float32)).astype(jnp.bfloat16)
    key_rows = projected[:, model_width : 2 * model_width].astype(jnp.bfloat16)
    value_rows = (projected[:, 2 * model_width :] + full_vbias.astype(jnp.float32)).astype(
        jnp.bfloat16
    )
    mixed_heads, logsums = lax.map(
        attend_sequence,
        (
            split_heads(queries),
            split_heads(key_rows),
            split_heads(value_rows),
            segment_ids,
            valid_mask,
        ),
    )
    mixed = mixed_heads.reshape(row_count, model_width)
    middle = (
        inputs
        + jnp.dot(mixed, full_proj, preferred_element_type=jnp.float32)
        + full_pbias.astype(jnp.float32)
    )
    normed2 = layer_norm(
        middle, full_gain2.astype(jnp.float32), full_bias2.astype(jnp.float32)
    ).astype(jnp.bfloat16)
    preact = jnp.dot(normed2, full_expand, preferred_element_type=jnp.float32) + full_ebias.astype(
        jnp.float32
    )
    activated = jax.nn.gelu(preact, approximate=False).astype(jnp.bfloat16)
    output = (
        middle
        + jnp.dot(activated, full_reduce, preferred_element_type=jnp.float32)
        + full_rbias.astype(jnp.float32)
    ).astype(jnp.bfloat16)
    back_gain1, back_qkv, back_proj, back_gain2, back_expand, back_reduce = (
        lax.all_gather(norm1_gain, "fsdp", axis=0, tiled=True),
        lax.all_gather(qkv_weight, "fsdp", axis=0, tiled=True),
        lax.all_gather(proj_weight, "fsdp", axis=0, tiled=True),
        lax.all_gather(norm2_gain, "fsdp", axis=0, tiled=True),
        lax.all_gather(expand_weight, "fsdp", axis=0, tiled=True),
        lax.all_gather(reduce_weight, "fsdp", axis=0, tiled=True),
    )
    zero_shift = jnp.zeros((model_width,), jnp.float32)
    grad_reduce = jnp.einsum("rk,rd->kd", activated, cotangent, preferred_element_type=jnp.float32)
    grad_rbias = jnp.sum(cotangent.astype(jnp.float32), axis=0)
    grad_activated = jnp.einsum(
        "rd,kd->rk", cotangent, back_reduce, preferred_element_type=jnp.float32
    )
    gelu_back = jax.vjp(partial(jax.nn.gelu, approximate=False), preact)[1]
    grad_preact = gelu_back(grad_activated)[0].astype(jnp.bfloat16)
    grad_expand = jnp.einsum("rd,rk->dk", normed2, grad_preact, preferred_element_type=jnp.float32)
    grad_ebias = jnp.sum(grad_preact.astype(jnp.float32), axis=0)
    grad_normed2 = jnp.einsum(
        "rk,dk->rd", grad_preact, back_expand, preferred_element_type=jnp.float32
    )
    norm2_back = jax.vjp(layer_norm, middle, back_gain2.astype(jnp.float32), zero_shift)[1]
    middle_part, grad_gain2, grad_bias2 = norm2_back(grad_normed2)
    grad_middle = cotangent.astype(jnp.float32) + middle_part
    grad_attended = grad_middle.astype(jnp.bfloat16)
    grad_proj = jnp.einsum("rd,re->de", mixed, grad_attended, preferred_element_type=jnp.float32)
    grad_pbias = jnp.sum(grad_attended.astype(jnp.float32), axis=0)
    grad_mixed = jnp.einsum(
        "re,de->rd", grad_attended, back_proj, preferred_element_type=jnp.float32
    ).astype(jnp.bfloat16)
    grad_qheads, grad_kheads, grad_vheads = lax.map(
        attend_back,
        (
            split_heads(queries),
            split_heads(key_rows),
            split_heads(value_rows),
            segment_ids,
            valid_mask,
            logsums,
            split_heads(grad_mixed),
        ),
    )
    grad_queries = grad_qheads.reshape(row_count, model_width)
    grad_keys = grad_kheads.reshape(row_count, model_width)
    grad_values = grad_vheads.reshape(row_count, model_width)
    grad_qbias = jnp.sum(grad_queries.astype(jnp.float32), axis=0)
    grad_vbias = jnp.sum(grad_values.astype(jnp.float32), axis=0)
    grad_projected = jnp.concatenate([grad_queries, grad_keys, grad_values], axis=1)
    grad_qkv = jnp.einsum("rd,rk->dk", normed1, grad_projected, preferred_element_type=jnp.float32)
    grad_normed1 = jnp.einsum(
        "rk,dk->rd", grad_projected, back_qkv, preferred_element_type=jnp.float32
    )
    norm1_back = jax.vjp(layer_norm, inputs, back_gain1.astype(jnp.float32), zero_shift)[1]
    input_part, grad_gain1, grad_bias1 = norm1_back(grad_normed1)
    input_grad = (grad_middle + input_part).astype(jnp.bfloat16)
    shards = (
        lax.psum_scatter(
            grad_gain1.astype(jnp.bfloat16), "fsdp", scatter_dimension=0, tiled=True
        ).astype(jnp.float32),
        lax.psum_scatter(
            grad_bias1.astype(jnp.bfloat16), "fsdp", scatter_dimension=0, tiled=True
        ).astype(jnp.float32),
        lax.psum_scatter(
            grad_qkv.astype(jnp.bfloat16), "fsdp", scatter_dimension=0, tiled=True
        ).astype(jnp.float32),
        lax.psum_scatter(
            grad_qbias.astype(jnp.bfloat16), "fsdp", scatter_dimension=0, tiled=True
        ).astype(jnp.float32),
        lax.psum_scatter(
            grad_vbias.astype(jnp.bfloat16), "fsdp", scatter_dimension=0, tiled=True
        ).astype(jnp.float32),
        lax.psum_scatter(
            grad_proj.astype(jnp.bfloat16), "fsdp", scatter_dimension=0, tiled=True
        ).astype(jnp.float32),
        lax.psum_scatter(
            grad_pbias.astype(jnp.bfloat16), "fsdp", scatter_dimension=0, tiled=True
        ).astype(jnp.float32),
        lax.psum_scatter(
            grad_gain2.astype(jnp.bfloat16), "fsdp", scatter_dimension=0, tiled=True
        ).astype(jnp.float32),
        lax.psum_scatter(
            grad_bias2.astype(jnp.bfloat16), "fsdp", scatter_dimension=0, tiled=True
        ).astype(jnp.float32),
        lax.psum_scatter(
            grad_expand.astype(jnp.bfloat16), "fsdp", scatter_dimension=0, tiled=True
        ).astype(jnp.float32),
        lax.psum_scatter(
            grad_ebias.astype(jnp.bfloat16), "fsdp", scatter_dimension=0, tiled=True
        ).astype(jnp.float32),
        lax.psum_scatter(
            grad_reduce.astype(jnp.bfloat16), "fsdp", scatter_dimension=0, tiled=True
        ).astype(jnp.float32),
        lax.psum_scatter(
            grad_rbias.astype(jnp.bfloat16), "fsdp", scatter_dimension=0, tiled=True
        ).astype(jnp.float32),
    )
    summed = (
        lax.psum(shards[0].astype(jnp.bfloat16), "rep").astype(jnp.float32),
        lax.psum(shards[1].astype(jnp.bfloat16), "rep").astype(jnp.float32),
        lax.psum(shards[2].astype(jnp.bfloat16), "rep").astype(jnp.float32),
        lax.psum(shards[3].astype(jnp.bfloat16), "rep").astype(jnp.float32),
        lax.psum(shards[4].astype(jnp.bfloat16), "rep").astype(jnp.float32),
        lax.psum(shards[5].astype(jnp.bfloat16), "rep").astype(jnp.float32),
        lax.psum(shards[6].astype(jnp.bfloat16), "rep").astype(jnp.float32),
        lax.psum(shards[7].astype(jnp.bfloat16), "rep").astype(jnp.float32),
        lax.psum(shards[8].astype(jnp.bfloat16), "rep").astype(jnp.float32),
        lax.psum(shards[9].astype(jnp.bfloat16), "rep").astype(jnp.float32),
        lax.psum(shards[10].astype(jnp.bfloat16), "rep").astype(jnp.float32),
        lax.psum(shards[11].astype(jnp.bfloat16), "rep").astype(jnp.float32),
        lax.psum(shards[12].astype(jnp.bfloat16), "rep").astype(jnp.float32),
    )
    (
        sum_gain1,
        sum_bias1,
        sum_qkv,
        sum_qbias,
        sum_vbias,
        sum_proj,
        sum_pbias,
        sum_gain2,
        sum_bias2,
        sum_expand,
        sum_ebias,
        sum_reduce,
        sum_rbias,
    ) = summed
    return (
        output,
        input_grad,
        sum_gain1,
        sum_bias1,
        sum_qkv,
        sum_qbias,
        sum_vbias,
        sum_proj,
        sum_pbias,
        sum_gain2,
        sum_bias2,
        sum_expand,
        sum_ebias,
        sum_reduce,
        sum_rbias,
    )


def solution(mesh):
    in_specs = (
        P(("rep", "fsdp"), None),
        P(("rep", "fsdp"), None),
        P(("rep", "fsdp"), None),
        P(("rep", "fsdp"), None),
        P("fsdp"),
        P("fsdp"),
        P("fsdp", None),
        P("fsdp"),
        P("fsdp"),
        P("fsdp", None),
        P("fsdp"),
        P("fsdp"),
        P("fsdp"),
        P("fsdp", None),
        P("fsdp"),
        P("fsdp", None),
        P("fsdp"),
    )
    out_specs = (
        P(("rep", "fsdp"), None),
        P(("rep", "fsdp"), None),
        P("fsdp"),
        P("fsdp"),
        P("fsdp", None),
        P("fsdp"),
        P("fsdp"),
        P("fsdp", None),
        P("fsdp"),
        P("fsdp"),
        P("fsdp"),
        P("fsdp", None),
        P("fsdp"),
        P("fsdp", None),
        P("fsdp"),
    )
    return jax.shard_map(local, mesh=mesh, in_specs=in_specs, out_specs=out_specs, check_vma=False)
```

profile of v0, /device:TPU:0, one launch (start us, length us, event | category | flops | bytes accessed | tf_op | source)
XLA Modules:
  0.0 1098.9 jit_solution(11289587286373675298)
XLA Ops:
  18.6 31.7 %all-reduce.18 = (bf16[768]{0:T(1024)(128)(2,1)S(1)}, bf16[768]{0:T(1024)(128)(2,1)S(1)}, bf16[768]{0:T(1024)(128)(2,1)S(1)}, bf16[768]{0:T(1024)(128)(2,1)S(1)}...) all-reduce(bf16[768]{0:T(1024)(128)(2,1)S(1)} %dynamic-update-slice, ...), channel_id=1, replica_groups=mesh['rep'=4,'fsdp'=8] {'fsdp'}, use_global_device_ids=true, to_apply=%add.1 | all-reduce | flops 5376 | bytes 21504
  52.0 12.7 %all-gather = bf16[8,1,384]{2,1,0:T(2,128)(2,1)S(1)} all-gather(bf16[1,1,384]{2,1,0:T(2,128)(2,1)S(1)} %reshape.404), channel_id=1, replica_groups=mesh['rep'=4,'fsdp'=8] {'fsdp'}, dimensions={0}, use_global_device_ids=true | all-gather | bytes 6912 | tf_op jit(solution)/shard_map/all_gather | solution.py:138
  75.5 10.1 fusion.119
  129.3 155.2 %while.26 = (s32[]{:T(128)}, bf16[2,1024,12,64]{1,3,2,0:T(8,128)(2,1)}, f32[2,12,1024,1]{2,1,3,0:T(8,128)S(1)}, bf16[2,1024,12,64]{1,3,2,0:T(8,128)(2,1)}, s32[2...) while((s32[]{:T(128)}, ...), condition=%wide.region_7.8_spmd, body=%wide.region_2.7_spmd.sunk | while | flops 3403416576 | bytes 243827504 | solution.py:174
  130.4 15.1 %fusion.185 = (f32[12,512]{1,0:T(8,128)S(1)}, f32[12,512,1024]{2,1,0:T(8,128)}) fusion(pred[512,1024]{1,0:T(8,128)(4,1)S(1)} %get-tuple-element.466, bf16[2,1024,12,64]{1,3,2,0:T(8,128)(2,1)} %get-tuple-element.526, s32[]{:T(128)S(6)} %copy.116, bf16[2,1024,12,64]{1,3,2,0:T(8,128)(2,1)} %get-tuple-element.525, s32[]{:T(128)S(6)} %add.336), kind=kOutput, calls=%fused_computation.7.clone.1 | convolution fusion | flops 824174592 | bytes 28075520 | tf_op jit(solution)/shard_map/while/body/eval_jaxpr/qhd,khd->hqk/dot_general | solution.py:24
  145.5 14.5 %fusion.186 = (f32[12,512]{1,0:T(8,128)S(1)}, f32[12,512,1024]{2,1,0:T(8,128)}) fusion(pred[512,1024]{1,0:T(8,128)(4,1)S(1)} %get-tuple-element.468, bf16[2,1024,12,64]{1,3,2,0:T(8,128)(2,1)} %get-tuple-element.526, s32[]{:T(128)S(6)} %copy.116, bf16[2,1024,12,64]{1,3,2,0:T(8,128)(2,1)} %get-tuple-element.525), kind=kOutput, calls=%fused_computation.6.clone.1 | convolution fusion | flops 824174592 | bytes 28075008 | tf_op jit(solution)/shard_map/while/body/eval_jaxpr/qhd,khd->hqk/dot_general | solution.py:24
  160.0 22.8 %fusion.187 = (f32[12,512]{1,0:T(8,128)S(1)}, f32[12,512]{1,0:T(8,128)S(1)}) fusion(f32[12,512,1024]{2,1,0:T(8,128)} %get-tuple-element.469, f32[12,512]{1,0:T(8,128)S(1)} %get-tuple-element.470, pred[512,1024]{1,0:T(8,128)(4,1)S(1)} %get-tuple-element.468, f32[12,512]{1,0:T(8,128)S(1)} %get-tuple-element.471, ...), kind=kLoop, calls=%fused_computation.8.clone.1 | loop fusion | flops 62902272 | bytes 51478528 | tf_op jit(solution)/shard_map/while/body/eval_jaxpr/reduce_sum | solution.py:47
  182.8 13.4 %fusion.189 = bf16[512,12,64]{0,2,1:T(8,128)(2,1)S(1)} fusion(f32[12,512,1024]{2,1,0:T(8,128)} %get-tuple-element.469, f32[12,512]{1,0:T(8,128)S(1)} %get-tuple-element.473, f32[12,512]{1,0:T(8,128)S(1)} %get-tuple-element.470, pred[512,1024]{1,0:T(8,128)(4,1)S(1)} %get-tuple-element.468, bf16[2,1024,12,64]{1,3,2,0:T(8,128)(2,1)} %get-tuple-element.522, ...), kind=kOutput, calls=%fused_computation.28.clone.1 | convolution fusion | flops 843448320 | bytes 28098564 | tf_op jit(solution)/shard_map/while/body/eval_jaxpr/hqk,khd->qhd/dot_general | solution.py:50
  196.3 9.7 fusion.188
  208.3 14.3 %fusion.185 = (f32[12,512]{1,0:T(8,128)S(1)}, f32[12,512,1024]{2,1,0:T(8,128)}) fusion(pred[512,1024]{1,0:T(8,128)(4,1)S(1)} %get-tuple-element.466, bf16[2,1024,12,64]{1,3,2,0:T(8,128)(2,1)} %get-tuple-element.526, s32[]{:T(128)S(6)} %copy.116, bf16[2,1024,12,64]{1,3,2,0:T(8,128)(2,1)} %get-tuple-element.525, s32[]{:T(128)S(6)} %add.336), kind=kOutput, calls=%fused_computation.7.clone.1 | convolution fusion | flops 824174592 | bytes 28075520 | tf_op jit(solution)/shard_map/while/body/eval_jaxpr/qhd,khd->hqk/dot_general | solution.py:24
  222.6 14.3 %fusion.186 = (f32[12,512]{1,0:T(8,128)S(1)}, f32[12,512,1024]{2,1,0:T(8,128)}) fusion(pred[512,1024]{1,0:T(8,128)(4,1)S(1)} %get-tuple-element.468, bf16[2,1024,12,64]{1,3,2,0:T(8,128)(2,1)} %get-tuple-element.526, s32[]{:T(128)S(6)} %copy.116, bf16[2,1024,12,64]{1,3,2,0:T(8,128)(2,1)} %get-tuple-element.525), kind=kOutput, calls=%fused_computation.6.clone.1 | convolution fusion | flops 824174592 | bytes 28075008 | tf_op jit(solution)/shard_map/while/body/eval_jaxpr/qhd,khd->hqk/dot_general | solution.py:24
  236.9 22.6 %fusion.187 = (f32[12,512]{1,0:T(8,128)S(1)}, f32[12,512]{1,0:T(8,128)S(1)}) fusion(f32[12,512,1024]{2,1,0:T(8,128)} %get-tuple-element.469, f32[12,512]{1,0:T(8,128)S(1)} %get-tuple-element.470, pred[512,1024]{1,0:T(8,128)(4,1)S(1)} %get-tuple-element.468, f32[12,512]{1,0:T(8,128)S(1)} %get-tuple-element.471, ...), kind=kLoop, calls=%fused_computation.8.clone.1 | loop fusion | flops 62902272 | bytes 51478528 | tf_op jit(solution)/shard_map/while/body/eval_jaxpr/reduce_sum | solution.py:47
  259.5 13.4 %fusion.189 = bf16[512,12,64]{0,2,1:T(8,128)(2,1)S(1)} fusion(f32[12,512,1024]{2,1,0:T(8,128)} %get-tuple-element.469, f32[12,512]{1,0:T(8,128)S(1)} %get-tuple-element.473, f32[12,512]{1,0:T(8,128)S(1)} %get-tuple-element.470, pred[512,1024]{1,0:T(8,128)(4,1)S(1)} %get-tuple-element.468, bf16[2,1024,12,64]{1,3,2,0:T(8,128)(2,1)} %get-tuple-element.522, ...), kind=kOutput, calls=%fused_computation.28.clone.1 | convolution fusion | flops 843448320 | bytes 28098564 | tf_op jit(solution)/shard_map/while/body/eval_jaxpr/hqk,khd->qhd/dot_general | solution.py:50
  273.0 9.7 fusion.188
  304.0 67.9 %multiply_convert_fusion.5 = (bf16[2048,3072]{1,0:T(8,128)(2,1)}, f32[2048,3072]{1,0:T(8,128)}, f32[2048,3072]{1,0:T(8,128)}) fusion(f32[3072]{0:T(1024)S(1)} %bitcast.286, bf16[768,3072]{1,0:T(8,128)(2,1)} %all-gather.10.cloned.1.call-done, bf16[2048,768]{0,1:T(8,128)(2,1)} %add_convert_fusion.6.clone.4), kind=kOutput, calls=%fused_computation.119 | convolution fusion | flops 10078912512 | bytes 70791168 | tf_op jit(solution)/shard_map/dot_general | solution.py:193
  371.9 28.2 %fusion.130 = (bf16[3072]{0:T(1024)(128)(2,1)}, bf16[2048,3072]{1,0:T(8,128)(2,1)}) fusion(f32[2048,3072]{1,0:T(8,128)} %get-tuple-element.301, bf16[2048,768]{1,0:T(8,128)(2,1)S(1)} %copy-done.11, bf16[3072,768]{1,0:T(8,128)(2,1)} %all-gather.12.cloned.1.call-done, f32[2048,3072]{1,0:T(8,128)} %get-tuple-element.330, f32[3072]{0:T(1024)S(1)} %bitcast.287), kind=kOutput, calls=%fused_computation.190 | convolution fusion | flops 9764336640 | bytes 70797312 | tf_op jit(solution)/shard_map/rd,kd->rk/dot_general | solution.py:213
  400.1 16.6 %fusion.129 = (bf16[768]{0:T(1024)(128)(2,1)}, f32[2048,768]{1,0:T(8,128)}) fusion(bf16[2048,3072]{1,0:T(8,128)(2,1)} %get-tuple-element.336, bf16[768,3072]{1,0:T(8,128)(2,1)} %all-gather.10.cloned.1.call-done), kind=kOutput, calls=%fused_computation.189 | convolution fusion | flops 9665248256 | bytes 23594496 | tf_op jit(solution)/shard_map/rk,dk->rd/dot_general | solution.py:220
  464.5 361.4 %while.27 = (s32[]{:T(128)}, bf16[2,1024,12,64]{1,3,2,0:T(8,128)(2,1)}, bf16[2,1024,12,64]{1,3,2,0:T(8,128)(2,1)}, bf16[2,1024,12,64]{1,3,2,0:T(8,128)(2,1)}, bf...) while((s32[]{:T(128)}, ...), condition=%wide.region_15.16_spmd, body=%wide.region_12.15_spmd.sunk | while | flops 8290292736 | bytes 519018368 | solution.py:232
  487.2 13.4 %fusion.203 = f32[12,512,1024]{2,1,0:T(8,128)} fusion(bf16[2,1024,12,64]{1,3,2,0:T(8,128)(2,1)} %get-tuple-element.562, s32[]{:T(128)S(6)} %copy.127, bf16[2,1024,12,64]{1,3,2,0:T(8,128)(2,1)} %get-tuple-element.565), kind=kOutput, calls=%fused_computation.77.clone.1 | convolution fusion | flops 805306368 | bytes 27526144 | tf_op jit(solution)/shard_map/while/body/eval_jaxpr/qhd,khd->hqk/dot_general | solution.py:24
  500.6 13.6 %fusion.202 = f32[12,512,1024]{2,1,0:T(8,128)} fusion(bf16[2,1024,12,64]{1,3,2,0:T(8,128)(2,1)} %get-tuple-element.562, s32[]{:T(128)S(6)} %copy.127, bf16[2,1024,12,64]{1,3,2,0:T(8,128)(2,1)} %get-tuple-element.565, s32[]{:T(128)S(6)} %add.340), kind=kOutput, calls=%fused_computation.73.clone.1 | convolution fusion | flops 805306368 | bytes 27526656 | tf_op jit(solution)/shard_map/while/body/eval_jaxpr/qhd,khd->hqk/dot_general | solution.py:24
  514.2 11.7 %fusion.208 = f32[12,64,1024]{2,1,0:T(8,128)S(1)} fusion(f32[12,512,1024]{2,1,0:T(8,128)} %fusion.202, f32[12,512]{1,0:T(8,128)S(1)} %get-tuple-element.485, pred[512,1024]{1,0:T(8,128)(4,1)S(1)} %get-tuple-element.488, bf16[2,1024,12,64]{1,3,2,0:T(8,128)(2,1)S(1)} %copy-done.14, s32[]{:T(128)S(6)} %copy.127, s32[]{:T(128)S(6)} %add.340), kind=kOutput, calls=%fused_computation.55.clone.1 | convolution fusion | flops 836763648 | bytes 29655048 | tf_op jit(solution)/shard_map/while/body/eval_jaxpr/hqk,qhd->khd/dot_general | solution.py:95
  525.8 13.3 %bitcast_dynamic-update-slice_fusion.5 = bf16[2,1024,12,64]{1,3,2,0:T(8,128)(2,1)} fusion(bf16[2,1024,12,64]{1,3,2,0:T(8,128)(2,1)} %get-tuple-element.547, s32[]{:T(128)S(6)} %copy.127, f32[12,64,1024]{2,1,0:T(8,128)S(1)} %fusion.208, f32[12,512]{1,0:T(8,128)S(1)} %get-tuple-element.491, f32[12,512,1024]{2,1,0:T(8,128)} %fusion.203, ...), kind=kOutput, calls=%fused_computation.65.clone.1 | convolution fusion | flops 838336512 | bytes 31228928 | tf_op jit(solution)/shard_map/while/body/eval_jaxpr/hqk,qhd->khd/dot_general | solution.py:95
  539.1 19.0 %multiply_reduce_fusion.7 = (f32[12,512]{1,0:T(8,128)S(1)}, f32[12,512,1024]{2,1,0:T(8,128)}) fusion(f32[12,512]{1,0:T(8,128)S(1)} %get-tuple-element.485, f32[12,512,1024]{2,1,0:T(8,128)} %fusion.202, pred[512,1024]{1,0:T(8,128)(4,1)S(1)} %get-tuple-element.488, bf16[2,1024,12,64]{1,3,2,0:T(8,128)(2,1)} %get-tuple-element.568, s32[]{:T(128)S(6)} %copy.127, ...), kind=kOutput, calls=%fused_computation.50.clone.1 | convolution fusion | flops 843048960 | bytes 53265920 | tf_op jit(solution)/shard_map/while/body/eval_jaxpr/qhd,khd->hqk/dot_general | solution.py:75
  558.1 19.1 %multiply_reduce_fusion.8 = (f32[12,512]{1,0:T(8,128)S(1)}, f32[12,512,1024]{2,1,0:T(8,128)}) fusion(f32[12,512]{1,0:T(8,128)S(1)} %get-tuple-element.491, f32[12,512,1024]{2,1,0:T(8,128)} %fusion.203, pred[512,1024]{1,0:T(8,128)(4,1)S(1)} %get-tuple-element.492, bf16[2,1024,12,64]{1,3,2,0:T(8,128)(2,1)} %get-tuple-element.568, s32[]{:T(128)S(6)} %copy.127, ...), kind=kOutput, calls=%fused_computation.53.clone.1 | convolution fusion | flops 843048960 | bytes 53265408 | tf_op jit(solution)/shard_map/while/body/eval_jaxpr/qhd,khd->hqk/dot_general | solution.py:75
  577.2 42.1 %multiply_convert_fusion.7 = (bf16[12,512,1024]{2,1,0:T(8,128)(2,1)}, bf16[12,512,1024]{2,1,0:T(8,128)(2,1)}) fusion(f32[12,512,1024]{2,1,0:T(8,128)} %get-tuple-element.489, f32[12,512]{1,0:T(8,128)S(1)} %get-tuple-element.490, f32[12,512]{1,0:T(8,128)S(1)} %get-tuple-element.485, f32[12,512,1024]{2,1,0:T(8,128)} %fusion.202, ...), kind=kLoop, calls=%fused_computation.49.clone.1 | loop fusion | flops 88080384 | bytes 126976000 | tf_op jit(solution)/shard_map/while/body/eval_jaxpr/convert_element_type | solution.py:79
  619.3 9.0 fusion.204
  628.3 9.1 fusion.205
  637.4 7.3 fusion.207
  652.7 13.4 %fusion.203 = f32[12,512,1024]{2,1,0:T(8,128)} fusion(bf16[2,1024,12,64]{1,3,2,0:T(8,128)(2,1)} %get-tuple-element.562, s32[]{:T(128)S(6)} %copy.127, bf16[2,1024,12,64]{1,3,2,0:T(8,128)(2,1)} %get-tuple-element.565), kind=kOutput, calls=%fused_computation.77.clone.1 | convolution fusion | flops 805306368 | bytes 27526144 | tf_op jit(solution)/shard_map/while/body/eval_jaxpr/qhd,khd->hqk/dot_general | solution.py:24
  666.1 13.5 %fusion.202 = f32[12,512,1024]{2,1,0:T(8,128)} fusion(bf16[2,1024,12,64]{1,3,2,0:T(8,128)(2,1)} %get-tuple-element.562, s32[]{:T(128)S(6)} %copy.127, bf16[2,1024,12,64]{1,3,2,0:T(8,128)(2,1)} %get-tuple-element.565, s32[]{:T(128)S(6)} %add.340), kind=kOutput, calls=%fused_computation.73.clone.1 | convolution fusion | flops 805306368 | bytes 27526656 | tf_op jit(solution)/shard_map/while/body/eval_jaxpr/qhd,khd->hqk/dot_general | solution.py:24
  679.7 11.7 %fusion.208 = f32[12,64,1024]{2,1,0:T(8,128)S(1)} fusion(f32[12,512,1024]{2,1,0:T(8,128)} %fusion.202, f32[12,512]{1,0:T(8,128)S(1)} %get-tuple-element.485, pred[512,1024]{1,0:T(8,128)(4,1)S(1)} %get-tuple-element.488, bf16[2,1024,12,64]{1,3,2,0:T(8,128)(2,1)S(1)} %copy-done.14, s32[]{:T(128)S(6)} %copy.127, s32[]{:T(128)S(6)} %add.340), kind=kOutput, calls=%fused_computation.55.clone.1 | convolution fusion | flops 836763648 | bytes 29655048 | tf_op jit(solution)/shard_map/while/body/eval_jaxpr/hqk,qhd->khd/dot_general | solution.py:95
  691.4 13.3 %bitcast_dynamic-update-slice_fusion.5 = bf16[2,1024,12,64]{1,3,2,0:T(8,128)(2,1)} fusion(bf16[2,1024,12,64]{1,3,2,0:T(8,128)(2,1)} %get-tuple-element.547, s32[]{:T(128)S(6)} %copy.127, f32[12,64,1024]{2,1,0:T(8,128)S(1)} %fusion.208, f32[12,512]{1,0:T(8,128)S(1)} %get-tuple-element.491, f32[12,512,1024]{2,1,0:T(8,128)} %fusion.203, ...), kind=kOutput, calls=%fused_computation.65.clone.1 | convolution fusion | flops 838336512 | bytes 31228928 | tf_op jit(solution)/shard_map/while/body/eval_jaxpr/hqk,qhd->khd/dot_general | solution.py:95
  704.7 19.0 %multiply_reduce_fusion.7 = (f32[12,512]{1,0:T(8,128)S(1)}, f32[12,512,1024]{2,1,0:T(8,128)}) fusion(f32[12,512]{1,0:T(8,128)S(1)} %get-tuple-element.485, f32[12,512,1024]{2,1,0:T(8,128)} %fusion.202, pred[512,1024]{1,0:T(8,128)(4,1)S(1)} %get-tuple-element.488, bf16[2,1024,12,64]{1,3,2,0:T(8,128)(2,1)} %get-tuple-element.568, s32[]{:T(128)S(6)} %copy.127, ...), kind=kOutput, calls=%fused_computation.50.clone.1 | convolution fusion | flops 843048960 | bytes 53265920 | tf_op jit(solution)/shard_map/while/body/eval_jaxpr/qhd,khd->hqk/dot_general | solution.py:75
  723.7 19.1 %multiply_reduce_fusion.8 = (f32[12,512]{1,0:T(8,128)S(1)}, f32[12,512,1024]{2,1,0:T(8,128)}) fusion(f32[12,512]{1,0:T(8,128)S(1)} %get-tuple-element.491, f32[12,512,1024]{2,1,0:T(8,128)} %fusion.203, pred[512,1024]{1,0:T(8,128)(4,1)S(1)} %get-tuple-element.492, bf16[2,1024,12,64]{1,3,2,0:T(8,128)(2,1)} %get-tuple-element.568, s32[]{:T(128)S(6)} %copy.127, ...), kind=kOutput, calls=%fused_computation.53.clone.1 | convolution fusion | flops 843048960 | bytes 53265408 | tf_op jit(solution)/shard_map/while/body/eval_jaxpr/qhd,khd->hqk/dot_general | solution.py:75
  742.8 42.1 %multiply_convert_fusion.7 = (bf16[12,512,1024]{2,1,0:T(8,128)(2,1)}, bf16[12,512,1024]{2,1,0:T(8,128)(2,1)}) fusion(f32[12,512,1024]{2,1,0:T(8,128)} %get-tuple-element.489, f32[12,512]{1,0:T(8,128)S(1)} %get-tuple-element.490, f32[12,512]{1,0:T(8,128)S(1)} %get-tuple-element.485, f32[12,512,1024]{2,1,0:T(8,128)} %fusion.202, ...), kind=kLoop, calls=%fused_computation.49.clone.1 | loop fusion | flops 88080384 | bytes 126976000 | tf_op jit(solution)/shard_map/while/body/eval_jaxpr/convert_element_type | solution.py:79
  784.9 9.0 fusion.204
  793.9 9.1 fusion.205
  803.0 7.3 fusion.207
  848.9 13.2 %convolution_convert_fusion.2 = bf16[768,2304]{1,0:T(8,128)(2,1)} fusion(bf16[2048,2304]{0,1:T(8,128)(2,1)} %constant_dynamic-update-slice_fusion, bf16[2048,768]{0,1:T(8,128)(2,1)S(1)} %copy-done.2, f32[768]{0:T(1024)S(1)} %copy-done.50, f32[768]{0:T(1024)S(1)} %copy-done.39, f32[2048]{0:T(1024)S(1)} %copy-done.31, f32[2048]{0:T(1024)S(1)} %copy-done.23), kind=kOutput, calls=%fused_computation.164 | convolution fusion | flops 7258963968 | bytes 16144384 | tf_op jit(solution)/shard_map/rd,rk->dk/dot_general | solution.py:250
  862.2 16.4 %convolution_convert_fusion.1 = bf16[768,3072]{1,0:T(8,128)(2,1)} fusion(bf16[2048,3072]{1,0:T(8,128)(2,1)} %get-tuple-element.336, f32[2048,768]{0,1:T(8,128)} %copy-done.4, f32[768]{0:T(1024)S(1)} %copy-done.44, f32[768]{0:T(1024)S(1)} %copy-done.42, f32[2048]{0:T(1024)S(1)} %copy-done.29, f32[2048]{0:T(1024)S(1)} %copy-done.26), kind=kOutput, calls=%fused_computation.163 | convolution fusion | flops 9673900032 | bytes 23615488 | tf_op jit(solution)/shard_map/rd,rk->dk/dot_general | solution.py:218
  878.7 15.5 %convolution_convert_fusion = bf16[3072,768]{1,0:T(8,128)(2,1)} fusion(bf16[2048,3072]{1,0:T(8,128)(2,1)} %get-tuple-element.300, bf16[2048,768]{1,0:T(8,128)(2,1)} %param.24), kind=kOutput, calls=%fused_computation.162 | convolution fusion | flops 9666035712 | bytes 20447232 | tf_op jit(solution)/shard_map/rk,rd->kd/dot_general | solution.py:211
  903.7 12.9 %fusion.128 = (bf16[768]{0:T(1024)(128)(2,1)S(1)}, f32[2048,768]{1,0:T(8,128)}) fusion(bf16[2048,2304]{0,1:T(8,128)(2,1)} %constant_dynamic-update-slice_fusion, bf16[768,2304]{1,0:T(8,128)(2,1)} %all-gather.6.cloned.1.call-done), kind=kOutput, calls=%fused_computation.188 | convolution fusion | flops 7249329152 | bytes 19269120 | tf_op jit(solution)/shard_map/rk,dk->rd/dot_general | solution.py:251
  931.1 28.8 %all-reduce.17 = (bf16[768]{0:T(1024)(128)(2,1)S(1)}, bf16[768]{0:T(1024)(128)(2,1)S(1)}, bf16[768]{0:T(1024)(128)(2,1)S(1)}, bf16[768]{0:T(1024)(128)(2,1)S(1)}...) all-reduce(bf16[768]{0:T(1024)(128)(2,1)S(1)} %dynamic-update-slice, ...), channel_id=1, replica_groups=mesh['rep'=4,'fsdp'=8] {'fsdp'}, use_global_device_ids=true, to_apply=%add.7 | all-reduce | flops 9984 | bytes 39936
  961.3 55.8 %reduce-scatter.11.cloned.1.call-done = bf16[384,768]{1,0:T(8,128)(2,1)} async-done(((bf16[3072,768]{1,0:T(8,128)(2,1)}), bf16[384,768]{1,0:T(8,128)(2,1)}) %reduce-scatter.11.cloned.1.call-update) | async-done | bytes 589840 | tf_op jit(solution)/shard_map/reduce_scatter | solution.py:291
  1017.1 16.5 %add_convert_fusion.3 = bf16[2048,768]{0,1:T(8,128)(2,1)} fusion(f32[2048,768]{0,1:T(8,128)} %copy-done.4, bf16[2048,3072]{1,0:T(8,128)(2,1)} %get-tuple-element.300, bf16[3072,768]{1,0:T(8,128)(2,1)} %all-gather.12.cloned.1.call-done, f32[768]{0:T(1024)S(1)} %convert_element_type.233), kind=kOutput, calls=%fused_computation.159 | convolution fusion | flops 9668395008 | bytes 26741760 | tf_op jit(solution)/shard_map/dot_general | solution.py:199
  1034.2 9.9 all-reduce.19
  1053.5 8.6 add_convert_fusion.2
  1066.7 17.5 %all-reduce.23.cloned.1.call-done = (bf16[96,2304]{1,0:T(8,128)(2,1)}, bf16[96,768]{1,0:T(8,128)(2,1)}, bf16[96,3072]{1,0:T(8,128)(2,1)}, bf16[384,768]{1,0:T(8,128)(2,1)}) async-done(((bf16[96,2304]{1,0:T(8,128)(2,1)}, bf16[96,768]{1,0:T(8,128)(2,1)}, bf16[96,3072]{1,0:T(8,128)(2,1)}, bf16[384,768]{1,0:T(8,128)(2,1)}), (bf16[96,2304]{1,0:T(8,128)(2,1)}, bf16[96,768]{1,0:T(8,128)(2,1)}, ...) | async-done | bytes 1769488 | tf_op jit(solution)/shard_map/psum | solution.py:301
  (330 shorter events, 224.1 us)
Async XLA Ops:
  7.2 68.4 %all-gather.6.cloned.1.call-start = ((), (), s32[]{:S(2)}) async-start(), calls=%async_computation.4 | async-start | bytes 3981312 | tf_op jit(solution)/shard_map/all_gather | solution.py:130
  7.9 284.6 %all-gather.8.cloned.1.call-start = ((), (), s32[]{:S(2)}) async-start(), calls=%async_computation.5 | async-start | bytes 1327104 | tf_op jit(solution)/shard_map/all_gather | solution.py:133
  8.7 295.3 %all-gather.10.cloned.1.call-start = ((), (), s32[]{:S(2)}) async-start(), calls=%async_computation.6 | async-start | bytes 5308416 | tf_op jit(solution)/shard_map/all_gather | solution.py:137
  9.4 362.5 %all-gather.12.cloned.1.call-start = ((), (), s32[]{:S(2)}) async-start(), calls=%async_computation.7 | async-start | bytes 5308416 | tf_op jit(solution)/shard_map/all_gather | solution.py:139
  10.0 950.0 %reduce-scatter.7.cloned.1.call-start = ((), (), s32[]{:S(2)}) async-start(), calls=%async_computation.9 | async-start | bytes 1327104 | tf_op jit(solution)/shard_map/reduce_scatter | solution.py:273
  50.2 25.3 %copy-start.49 = (f32[768]{0:T(1024)}, f32[768]{0:T(1024)S(1)}, u32[]{:S(2)}) copy-start(f32[768]{0:T(1024)S(1)} %convert_element_type.221) | copy-start | bytes 9220
  50.3 25.3 %copy-start.38 = (f32[768]{0:T(1024)}, f32[768]{0:T(1024)S(1)}, u32[]{:S(2)}) copy-start(f32[768]{0:T(1024)S(1)} %convert_element_type.220) | copy-start | bytes 9220
  69.3 16.3 %copy-start.22 = (f32[2048]{0:T(1024)}, f32[2048]{0:T(1024)S(1)}, u32[]{:S(2)}) copy-start(f32[2048]{0:T(1024)S(1)} %broadcast_multiply_fusion.1) | copy-start | bytes 24580
  70.8 14.8 %copy-start.30 = (f32[2048]{0:T(1024)}, f32[2048]{0:T(1024)S(1)}, u32[]{:S(2)}) copy-start(f32[2048]{0:T(1024)S(1)} %fusion.116) | copy-start | bytes 24580
  160.0 36.2 %slice-start.3 = ((s8[25165824]{0:T(1024)(128)(4,1)}), s8[4194304]{0:T(1024)(128)(4,1)S(1)}, s32[]{:S(2)}) async-start(s8[25165824]{0:T(1024)(128)(4,1)} %bitcast.267), calls=%async_computation.16 | async-start | bytes 8388608 | tf_op jit(solution)/shard_map/while
  160.0 36.2 %slice-start.4 = ((s8[25165824]{0:T(1024)(128)(4,1)}), s8[4194304]{0:T(1024)(128)(4,1)S(1)}, s32[]{:S(2)}) async-start(s8[25165824]{0:T(1024)(128)(4,1)} %bitcast.267), calls=%async_computation.17 | async-start | bytes 8388608 | tf_op jit(solution)/shard_map/while
  182.8 13.5 %slice-start.5 = ((s8[25165824]{0:T(1024)(128)(4,1)}), s8[4194304]{0:T(1024)(128)(4,1)S(1)}, s32[]{:S(2)}) async-start(s8[25165824]{0:T(1024)(128)(4,1)} %bitcast.267), calls=%async_computation.18 | async-start | bytes 8388608 | tf_op jit(solution)/shard_map/while
  182.8 13.5 %slice-start.6 = ((s8[25165824]{0:T(1024)(128)(4,1)}), s8[4194304]{0:T(1024)(128)(4,1)S(1)}, s32[]{:S(2)}) async-start(s8[25165824]{0:T(1024)(128)(4,1)} %bitcast.267), calls=%async_computation.19 | async-start | bytes 8388608 | tf_op jit(solution)/shard_map/while
  182.8 13.5 %slice-start.7 = ((s8[25165824]{0:T(1024)(128)(4,1)}), s8[4194304]{0:T(1024)(128)(4,1)S(1)}, s32[]{:S(2)}) async-start(s8[25165824]{0:T(1024)(128)(4,1)} %bitcast.267), calls=%async_computation.20 | async-start | bytes 8388608 | tf_op jit(solution)/shard_map/while
  182.8 13.5 %slice-start.8 = ((s8[25165824]{0:T(1024)(128)(4,1)}), s8[4194304]{0:T(1024)(128)(4,1)S(1)}, s32[]{:S(2)}) async-start(s8[25165824]{0:T(1024)(128)(4,1)} %bitcast.267), calls=%async_computation.21 | async-start | bytes 8388608 | tf_op jit(solution)/shard_map/while
  236.9 36.0 %slice-start.3 = ((s8[25165824]{0:T(1024)(128)(4,1)}), s8[4194304]{0:T(1024)(128)(4,1)S(1)}, s32[]{:S(2)}) async-start(s8[25165824]{0:T(1024)(128)(4,1)} %bitcast.267), calls=%async_computation.16 | async-start | bytes 8388608 | tf_op jit(solution)/shard_map/while
  236.9 36.0 %slice-start.4 = ((s8[25165824]{0:T(1024)(128)(4,1)}), s8[4194304]{0:T(1024)(128)(4,1)S(1)}, s32[]{:S(2)}) async-start(s8[25165824]{0:T(1024)(128)(4,1)} %bitcast.267), calls=%async_computation.17 | async-start | bytes 8388608 | tf_op jit(solution)/shard_map/while
  259.4 13.5 %slice-start.5 = ((s8[25165824]{0:T(1024)(128)(4,1)}), s8[4194304]{0:T(1024)(128)(4,1)S(1)}, s32[]{:S(2)}) async-start(s8[25165824]{0:T(1024)(128)(4,1)} %bitcast.267), calls=%async_computation.18 | async-start | bytes 8388608 | tf_op jit(solution)/shard_map/while
  259.4 13.5 %slice-start.6 = ((s8[25165824]{0:T(1024)(128)(4,1)}), s8[4194304]{0:T(1024)(128)(4,1)S(1)}, s32[]{:S(2)}) async-start(s8[25165824]{0:T(1024)(128)(4,1)} %bitcast.267), calls=%async_computation.19 | async-start | bytes 8388608 | tf_op jit(solution)/shard_map/while
  259.5 13.5 %slice-start.7 = ((s8[25165824]{0:T(1024)(128)(4,1)}), s8[4194304]{0:T(1024)(128)(4,1)S(1)}, s32[]{:S(2)}) async-start(s8[25165824]{0:T(1024)(128)(4,1)} %bitcast.267), calls=%async_computation.20 | async-start | bytes 8388608 | tf_op jit(solution)/shard_map/while
  259.5 13.5 %slice-start.8 = ((s8[25165824]{0:T(1024)(128)(4,1)}), s8[4194304]{0:T(1024)(128)(4,1)S(1)}, s32[]{:S(2)}) async-start(s8[25165824]{0:T(1024)(128)(4,1)} %bitcast.267), calls=%async_computation.21 | async-start | bytes 8388608 | tf_op jit(solution)/shard_map/while
  284.5 8.0 copy-start.16
  284.5 8.0 copy-start.1
  284.5 8.0 copy-start.51
  304.0 67.9 %copy-start.11 = (bf16[2048,768]{1,0:T(8,128)(2,1)S(1)}, bf16[2048,768]{1,0:T(8,128)(2,1)}, u32[]{:S(2)}) copy-start(bf16[2048,768]{1,0:T(8,128)(2,1)} %param.24) | copy-start | bytes 9437188
  416.6 13.7 %slice-start.9 = ((s8[6291456]{0:T(1024)(128)(4,1)}), s8[2097152]{0:T(1024)(128)(4,1)S(1)}, s32[]{:S(2)}) async-start(s8[6291456]{0:T(1024)(128)(4,1)} %bitcast.269), calls=%async_computation.22 | async-start | bytes 4194304
  423.4 6.9 copy-start.37
  423.4 6.9 slice-start.10
  423.4 7.7 copy-start.6
  441.3 518.6 %reduce-scatter.5.cloned.1.call-start = ((), (), s32[]{:S(2)}) async-start(), calls=%async_computation.8 | async-start | bytes 3981312 | tf_op jit(solution)/shard_map/reduce_scatter | solution.py:264
  500.6 13.6 %copy-start.14 = (bf16[2,1024,12,64]{1,3,2,0:T(8,128)(2,1)S(1)}, bf16[2,1024,12,64]{1,3,2,0:T(8,128)(2,1)}, u32[]{:S(2)}) copy-start(bf16[2,1024,12,64]{1,3,2,0:T(8,128)(2,1)} %get-tuple-element.567) | copy-start | bytes 9437188 | tf_op jit(solution)/shard_map/while
  628.3 16.4 %slice-start = ((s8[12582912]{0:T(1024)(128)(4,1)}), s8[4194304]{0:T(1024)(128)(4,1)S(1)}, s32[]{:S(2)}) async-start(s8[12582912]{0:T(1024)(128)(4,1)} %bitcast.265), calls=%async_computation.13 | async-start | bytes 8388608 | tf_op jit(solution)/shard_map/while
  628.3 16.4 %slice-start.1 = ((s8[12582912]{0:T(1024)(128)(4,1)}), s8[4194304]{0:T(1024)(128)(4,1)S(1)}, s32[]{:S(2)}) async-start(s8[12582912]{0:T(1024)(128)(4,1)} %bitcast.265), calls=%async_computation.14 | async-start | bytes 8388608 | tf_op jit(solution)/shard_map/while
  637.4 7.3 slice-start.2
  637.4 7.3 copy-start.12
  666.1 13.6 %copy-start.14 = (bf16[2,1024,12,64]{1,3,2,0:T(8,128)(2,1)S(1)}, bf16[2,1024,12,64]{1,3,2,0:T(8,128)(2,1)}, u32[]{:S(2)}) copy-start(bf16[2,1024,12,64]{1,3,2,0:T(8,128)(2,1)} %get-tuple-element.567) | copy-start | bytes 9437188 | tf_op jit(solution)/shard_map/while
  793.9 16.4 %slice-start = ((s8[12582912]{0:T(1024)(128)(4,1)}), s8[4194304]{0:T(1024)(128)(4,1)S(1)}, s32[]{:S(2)}) async-start(s8[12582912]{0:T(1024)(128)(4,1)} %bitcast.265), calls=%async_computation.13 | async-start | bytes 8388608 | tf_op jit(solution)/shard_map/while
  793.9 16.4 %slice-start.1 = ((s8[12582912]{0:T(1024)(128)(4,1)}), s8[4194304]{0:T(1024)(128)(4,1)S(1)}, s32[]{:S(2)}) async-start(s8[12582912]{0:T(1024)(128)(4,1)} %bitcast.265), calls=%async_computation.14 | async-start | bytes 8388608 | tf_op jit(solution)/shard_map/while
  803.0 7.3 slice-start.2
  803.0 7.3 copy-start.12
  848.9 13.3 %copy-start.26 = (f32[2048]{0:T(1024)S(1)}, f32[2048]{0:T(1024)}, u32[]{:S(2)}) copy-start(f32[2048]{0:T(1024)} %copy-done.24) | copy-start | bytes 24580
  848.9 13.3 %copy-start.29 = (f32[2048]{0:T(1024)S(1)}, f32[2048]{0:T(1024)}, u32[]{:S(2)}) copy-start(f32[2048]{0:T(1024)} %copy-done.27) | copy-start | bytes 24580
  848.9 13.3 %copy-start.42 = (f32[768]{0:T(1024)S(1)}, f32[768]{0:T(1024)}, u32[]{:S(2)}) copy-start(f32[768]{0:T(1024)} %convert_element_type.228) | copy-start | bytes 9220
  848.9 13.3 %copy-start.44 = (f32[768]{0:T(1024)S(1)}, f32[768]{0:T(1024)}, u32[]{:S(2)}) copy-start(f32[768]{0:T(1024)} %convert_element_type.229) | copy-start | bytes 9220
  862.2 99.1 %reduce-scatter.9.cloned.1.call-start = ((), (), s32[]{:S(2)}) async-start(), calls=%async_computation.10 | async-start | bytes 5308416 | tf_op jit(solution)/shard_map/reduce_scatter | solution.py:285
  878.6 138.4 %reduce-scatter.11.cloned.1.call-start = ((), (), s32[]{:S(2)}) async-start(), calls=%async_computation.11 | async-start | bytes 5308416 | tf_op jit(solution)/shard_map/reduce_scatter | solution.py:291
  894.2 190.0 %all-reduce.23.cloned.1.call-start = ((), (), s32[]{:S(2)}) async-start(), calls=%async_computation.12 | async-start | bytes 3538944 | tf_op jit(solution)/shard_map/psum | solution.py:301
  1033.5 20.0 %copy-start.33 = (f32[2048]{0:T(1024)S(1)}, f32[2048]{0:T(1024)}, u32[]{:S(2)}) copy-start(f32[2048]{0:T(1024)} %copy-done.32) | copy-start | bytes 24580
  (40 other events, 157.7 us)
Sparse Core Ops, SparseCore 0:
  9.7 44.9 all-gather.5
  56.3 21.3 all-gather.7
  79.4 51.4 all-gather.9
  132.4 50.5 all-gather.11
  441.4 31.2 reduce-scatter.6
  862.3 42.4 reduce-scatter.4
  907.2 54.0 reduce-scatter.8
  963.7 53.3 reduce-scatter.10
  1020.9 63.2 all-reduce.22
where the time goes:
time: 1100 us
  matrix products  554 us (50%)
  other arithmetic  193 us (18%)
  local copies, waits for them, and re-layouts  143 us (13%)
  blocking collectives  83.1 us (8%)
  waiting for transfers between devices  77.3 us (7%)
  loops' own time  31.3 us (3%)
  between operations  16.6 us (2%)
    dot_general x8, matrix products, block_scores(): jnp.einsum('qhd,khd->hqk', query_rows, key_heads, preferred_element_type=...  112 us
    convert_element_type x2, other arithmetic, attend_back(): grad_scores = (probs * (grad_probs - inner)).astype(jnp.bfloat16)  84.1 us
    dot_general x4, matrix products, attend_back(): jnp.einsum('qhd,khd->hqk', grad_rows, value_heads, preferred_element_type...  76.2 us
    dot_general x1, matrix products, local(): jnp.dot(normed2, full_expand, preferred_element_type=jnp.float32)  67.9 us
    unnamed x2, blocking collectives  60.5 us
    reduce_scatter x1, waiting for transfers between devices, local(): lax.psum_scatter(grad_reduce.astype(jnp.bfloat16), 'fsdp', scatter_dimens...  55.8 us
    dot_general x4, matrix products, attend_back(): jnp.einsum('hqk,qhd->khd', probs.astype(jnp.bfloat16), grad_rows, preferr...  50 us
    dot_general x4, matrix products, attend_sequence(): jnp.einsum('hqk,khd->qhd', attn_weights, value_heads, preferred_element_t...  46.3 us
  transfers between devices with their start and end apart: 9, of which 3 were waited for; matrix products, arithmetic and copies ran while one was open for 73% of the time, Pallas kernels for 0%

commit v1 on v0

v1 whole, which is shorter than its diff:
```python
import functools

import jax
import jax.numpy as jnp
from jax import lax
from jax.experimental import pallas as pl
from jax.experimental.pallas import tpu as pltpu
from jax.sharding import PartitionSpec as P

HEADS = 12
CLIPS = 6
EPSILON = 1e-06
WINDOW = 256
FIELDS = 5
BF16 = jnp.bfloat16
F32 = jnp.float32
MEBI = 1024 * 1024
NEGATIVE = -1e30


def dot(left, right):
    return lax.dot_general(left, right, (((1,), (0,)), ((), ())), preferred_element_type=F32)


def dot_nt(left, right):
    return lax.dot_general(left, right, (((1,), (1,)), ((), ())), preferred_element_type=F32)


def dot_tn(left, right):
    return lax.dot_general(left, right, (((0,), (0,)), ((), ())), preferred_element_type=F32)


def resident(shape):
    zeros = (0,) * len(shape)
    return pl.BlockSpec(shape, lambda *_: zeros, pipeline_mode=pl.Buffered(1))


def params(limit, count=1):
    return pltpu.CompilerParams(
        vmem_limit_bytes=limit * MEBI, dimension_semantics=("arbitrary",) * count
    )


def normalise(values):
    row_mean = jnp.mean(values, axis=-1, keepdims=True)
    centred = values - row_mean
    row_var = jnp.mean(centred * centred, axis=-1, keepdims=True)
    scale = lax.rsqrt(row_var + EPSILON)
    return centred * scale, scale


def norm_back(upstream, gain, xhat, scale):
    weighted = upstream * gain
    first = jnp.mean(weighted, axis=-1, keepdims=True)
    second = jnp.mean(weighted * xhat, axis=-1, keepdims=True)
    return scale * (weighted - first - xhat * second)


def qkv_kernel(tokens, vecs, weight, qkv, normed):
    width = tokens.shape[1]
    xhat, _ = normalise(tokens[...].astype(F32))
    rows = (xhat * vecs[0:1, :] + vecs[1:2, :]).astype(BF16)
    normed[...] = rows
    query = dot(rows, weight[:, :width]) + vecs[2:3, :]
    qkv[:, :width] = query.astype(BF16) * jnp.asarray(0.125, BF16)
    qkv[:, width : 2 * width] = dot(rows, weight[:, width : 2 * width]).astype(BF16)
    value = dot(rows, weight[:, 2 * width :]) + vecs[3:4, :]
    qkv[:, 2 * width :] = value.astype(BF16)


def qkv_forward(tokens, vecs, weight, block=512):
    rows, width = tokens.shape
    return pl.pallas_call(
        qkv_kernel,
        grid=(rows // block,),
        in_specs=[
            pl.BlockSpec((block, width), lambda i: (i, 0)),
            resident(vecs.shape),
            resident(weight.shape),
        ],
        out_specs=[
            pl.BlockSpec((block, 3 * width), lambda i: (i, 0)),
            pl.BlockSpec((block, width), lambda i: (i, 0)),
        ],
        out_shape=[
            jax.ShapeDtypeStruct((rows, 3 * width), BF16),
            jax.ShapeDtypeStruct((rows, width), BF16),
        ],
        compiler_params=params(40),
    )(tokens, vecs, weight)


def clip_table(segment_ids, valid_mask):
    seq_len = segment_ids.shape[1]
    clips = jnp.arange(CLIPS, dtype=jnp.int32)[None, :, None]
    segments = segment_ids[:, None, :]
    start = jnp.sum((segments < clips).astype(jnp.int32), axis=2)
    end = jnp.sum((segments <= clips).astype(jnp.int32), axis=2)
    valid = jnp.sum(((segments == clips) & (valid_mask[:, None, :] == 1)).astype(jnp.int32), axis=2)
    aligned = start // 16 * 16
    need = end - aligned
    path = (need > WINDOW).astype(jnp.int32) + (need > 2 * WINDOW).astype(jnp.int32)
    window = jnp.where(path == 0, WINDOW, jnp.where(path == 1, 2 * WINDOW, seq_len))
    base = jnp.minimum(aligned, seq_len - window)
    return jnp.stack([base, path, start - base, end - base, start + valid - base], axis=2).reshape(
        -1
    )


def lane_low(rows):
    return lax.broadcasted_iota(jnp.int32, (rows, 128), 1) < 64


def flag_lane(rows):
    return lax.broadcasted_iota(jnp.int32, (rows, 128), 1) % 64 == 0


def row_mask(rows, offset, first, last):
    index = lax.broadcasted_iota(jnp.int32, (rows, 128), 0) + offset
    return (index >= first) & (index < last)


def key_extra(rows, first, last):
    bias = jnp.where(row_mask(rows, 0, first, last), 0.0, NEGATIVE)
    return jnp.where(flag_lane(rows), bias, 0.0).astype(BF16)


def query_extra(rows):
    return jnp.where(flag_lane(rows), 1.0, 0.0).astype(BF16)


def weights_of(query, keys, extra_query, extra_keys, low, low_keys, head):
    if head == 0:
        left = jnp.where(low, query, extra_query)
        right = jnp.where(low_keys, keys, extra_keys)
    else:
        left = jnp.where(low, extra_query, query)
        right = jnp.where(low_keys, extra_keys, keys)
    scores = dot_nt(left, right)
    return jnp.exp(scores - jnp.max(scores, axis=1, keepdims=True)).astype(BF16)


def attend_window(refs, base, first, last, valid_end, window, pairs, exps, clip):
    queries, keys_ref, values_ref, mixed, inverse = refs
    chunk = WINDOW
    low = lane_low(chunk)
    low_keys = lane_low(window)
    extra_keys = key_extra(window, first, valid_end)
    extra_query = query_extra(chunk)
    ones = jnp.ones((window, 128), BF16)
    key_rows = pl.ds(base, window)

    def one_chunk(offset, row_start):
        rows = pl.ds(row_start, chunk)
        keep = row_mask(chunk, offset, first, last)
        for pair in range(pairs):
            lanes = pl.ds(128 * pair, 128)
            query = queries[rows, lanes]
            keys = keys_ref[key_rows, lanes]
            stack = jnp.concatenate([values_ref[key_rows, lanes], ones], axis=1)
            sums = []
            for head in range(2):
                weights = weights_of(query, keys, extra_query, extra_keys, low, low_keys, head)
                if exps is not None:
                    exps[0, 2 * pair + head, pl.ds(clip * WINDOW, WINDOW), :] = weights
                sums.append(dot(weights, stack))
            total = jnp.where(low, sums[0][:, 128:], sums[1][:, 128:])
            weighted = jnp.where(low, sums[0][:, :128], sums[1][:, :128])
            reciprocal = 1.0 / total
            mixed[rows, lanes] = jnp.where(
                keep, (weighted * reciprocal), mixed[rows, lanes].astype(F32)
            ).astype(BF16)
            inverse[rows, lanes] = jnp.where(keep, reciprocal, inverse[rows, lanes])

    if window == chunk:
        one_chunk(0, base)
    else:

        def step(index, carry):
            offset = index * chunk
            one_chunk(offset, pl.multiple_of(base + offset, 16))
            return carry

        lax.fori_loop(0, window // chunk, step, 0)


def clip_fields(table, sequence, clip):
    at = (sequence * CLIPS + clip) * FIELDS
    base = pl.multiple_of(table[at], 16)
    return base, table[at + 1], table[at + 2], table[at + 3], table[at + 4]


def attend_kernel(pairs, table, queries, keys, values, mixed, inverse, exps):
    sequence = pl.program_id(0)
    seq_len = queries.shape[0]
    mixed[...] = jnp.zeros_like(mixed)
    inverse[...] = jnp.zeros_like(inverse)
    refs = (queries, keys, values, mixed, inverse)

    def one_clip(clip, carry):
        base, path, first, last, valid_end = clip_fields(table, sequence, clip)
        for number, window in enumerate((WINDOW, 2 * WINDOW, seq_len)):

            @pl.when(path == number)
            def _():
                attend_window(
                    refs,
                    base,
                    first,
                    last,
                    valid_end,
                    window,
                    pairs,
                    exps if number == 0 else None,
                    clip,
                )

        return carry

    lax.fori_loop(0, CLIPS, one_clip, 0)


def attend_forward(table, qkv, seq_len, pairs=2):
    rows = qkv.shape[0]
    width = qkv.shape[1] // 3
    seqs = rows // seq_len
    lanes = 128 * pairs
    groups = width // lanes
    block = (seq_len, lanes)
    return pl.pallas_call(
        functools.partial(attend_kernel, pairs),
        grid_spec=pltpu.PrefetchScalarGridSpec(
            num_scalar_prefetch=1,
            grid=(seqs, groups),
            in_specs=[
                pl.BlockSpec(block, lambda s, g, t: (s, g)),
                pl.BlockSpec(block, lambda s, g, t: (s, groups + g)),
                pl.BlockSpec(block, lambda s, g, t: (s, 2 * groups + g)),
            ],
            out_specs=[
                pl.BlockSpec(block, lambda s, g, t: (s, g)),
                pl.BlockSpec(block, lambda s, g, t: (s, g)),
                pl.BlockSpec((1, 2 * pairs, CLIPS * WINDOW, WINDOW), lambda s, g, t: (s, g, 0, 0)),
            ],
        ),
        out_shape=[
            jax.ShapeDtypeStruct((rows, width), BF16),
            jax.ShapeDtypeStruct((rows, width), F32),
            jax.ShapeDtypeStruct((seqs, HEADS, CLIPS * WINDOW, WINDOW), BF16),
        ],
        compiler_params=params(48, 2),
    )(table, qkv, qkv, qkv)


def back_window(refs, base, first, last, valid_end, window, pairs, exps, clip, gather):
    queries, keys_ref, values_ref, grads, mixed, inverse, dq, dk, dv = refs
    key_grad, value_grad = gather
    chunk = WINDOW
    single = window == chunk
    low = lane_low(chunk)
    low_keys = lane_low(window)
    extra_keys = None if single else key_extra(window, first, valid_end)
    extra_query = None if single else query_extra(chunk)
    key_rows = pl.ds(base, window)
    one = jnp.ones((window, 128), BF16)

    def one_chunk(offset, row_start):
        rows = pl.ds(row_start, chunk)
        keep = row_mask(chunk, offset, first, last)
        for pair in range(pairs):
            lanes = pl.ds(128 * pair, 128)
            query = queries[rows, lanes]
            keys = keys_ref[key_rows, lanes]
            values = values_ref[key_rows, lanes]
            scaled = jnp.where(keep, grads[rows, lanes].astype(F32) * inverse[rows, lanes], 0.0)
            product = scaled * mixed[rows, lanes].astype(F32)
            turned = pltpu.roll(-product, 64, 1).astype(BF16)
            scaled = scaled.astype(BF16)
            parts = []
            for head in range(2):
                if head == 0:
                    left = jnp.where(low, scaled, turned)
                    right = jnp.where(low_keys, values, one)
                else:
                    left = jnp.where(low, turned, scaled)
                    right = jnp.where(low_keys, one, values)
                if single:
                    weights = exps[0, 2 * pair + head, pl.ds(clip * WINDOW, WINDOW), :]
                else:
                    weights = weights_of(query, keys, extra_query, extra_keys, low, low_keys, head)
                grad_scores = (weights.astype(F32) * dot_nt(left, right)).astype(BF16)
                parts.append(
                    (
                        dot(grad_scores, keys),
                        dot_tn(grad_scores, query),
                        dot_tn(weights, scaled),
                    )
                )
            query_part = jnp.where(low, parts[0][0], parts[1][0]) * 0.125
            key_part = jnp.where(low_keys, parts[0][1], parts[1][1])
            value_part = jnp.where(low_keys, parts[0][2], parts[1][2])
            dq[rows, lanes] = jnp.where(keep, query_part, dq[rows, lanes].astype(F32)).astype(BF16)
            if single:
                dk[rows, lanes] = jnp.where(keep, key_part, dk[rows, lanes].astype(F32)).astype(
                    BF16
                )
                dv[rows, lanes] = jnp.where(keep, value_part, dv[rows, lanes].astype(F32)).astype(
                    BF16
                )
            else:
                key_grad[pl.ds(0, window), lanes] += key_part
                value_grad[pl.ds(0, window), lanes] += value_part

    if single:
        one_chunk(0, base)
        return
    key_grad[...] = jnp.zeros_like(key_grad)
    value_grad[...] = jnp.zeros_like(value_grad)

    def step(index, carry):
        offset = index * chunk
        one_chunk(offset, pl.multiple_of(base + offset, 16))
        return carry

    lax.fori_loop(0, window // chunk, step, 0)
    keep = row_mask(window, 0, first, last)
    for pair in range(pairs):
        lanes = pl.ds(128 * pair, 128)
        for ref, total in ((dk, key_grad), (dv, value_grad)):
            ref[key_rows, lanes] = jnp.where(
                keep, total[pl.ds(0, window), lanes], ref[key_rows, lanes].astype(F32)
            ).astype(BF16)


def back_kernel(
    pairs,
    table,
    queries,
    keys,
    values,
    grads,
    mixed,
    inverse,
    exps,
    dq,
    dk,
    dv,
    key_grad,
    value_grad,
):
    sequence = pl.program_id(0)
    seq_len = queries.shape[0]
    for ref in (dq, dk, dv):
        ref[...] = jnp.zeros_like(ref)
    refs = (queries, keys, values, grads, mixed, inverse, dq, dk, dv)

    def one_clip(clip, carry):
        base, path, first, last, valid_end = clip_fields(table, sequence, clip)
        for number, window in enumerate((WINDOW, 2 * WINDOW, seq_len)):

            @pl.when(path == number)
            def _():
                back_window(
                    refs,
                    base,
                    first,
                    last,
                    valid_end,
                    window,
                    pairs,
                    exps,
                    clip,
                    (key_grad, value_grad),
                )

        return carry

    lax.fori_loop(0, CLIPS, one_clip, 0)


def attend_backward(table, qkv, grads, mixed, inverse, exps, seq_len, pairs=2):
    rows, width = mixed.shape
    seqs = rows // seq_len
    lanes = 128 * pairs
    groups = width // lanes
    block = (seq_len, lanes)
    own = pl.BlockSpec(block, lambda s, g, t: (s, g))
    shape = jax.ShapeDtypeStruct((rows, width), BF16)
    return pl.pallas_call(
        functools.partial(back_kernel, pairs),
        grid_spec=pltpu.PrefetchScalarGridSpec(
            num_scalar_prefetch=1,
            grid=(seqs, groups),
            in_specs=[
                own,
                pl.BlockSpec(block, lambda s, g, t: (s, groups + g)),
                pl.BlockSpec(block, lambda s, g, t: (s, 2 * groups + g)),
                own,
                own,
                own,
                pl.BlockSpec((1, 2 * pairs, CLIPS * WINDOW, WINDOW), lambda s, g, t: (s, g, 0, 0)),
            ],
            out_specs=[own, own, own],
            scratch_shapes=[pltpu.VMEM(block, F32), pltpu.VMEM(block, F32)],
        ),
        out_shape=[shape, shape, shape],
        compiler_params=params(48, 2),
    )(table, qkv, qkv, qkv, grads, mixed, inverse, exps)


def gauss(value):
    size = jnp.abs(value)
    rate = 1.0 / (1.0 + 0.3275911 * 0.7071067811865476 * size)
    tail = jnp.exp(value * value * -0.5)
    series = rate * (
        0.5 * 0.254829592
        + rate
        * (
            0.5 * -0.284496736
            + rate * (0.5 * 1.421413741 + rate * (0.5 * -1.453152027 + rate * (0.5 * 1.061405429)))
        )
    )
    upper = series * tail
    return jnp.where(value >= 0, 1.0 - upper, upper), value * tail * 0.3989422804014327


def middle_kernel(
    part,
    tokens,
    mixed,
    cotangent,
    vecs,
    ebias,
    proj,
    expand,
    reduce,
    output,
    grad_middle,
    grad_mixed,
    grad_proj,
    grad_expand,
    grad_reduce,
    grad_ebias,
    grad_vecs,
    sum_proj,
    sum_expand,
    sum_reduce,
):
    step = pl.program_id(0)
    hidden = expand.shape[1]

    @pl.when(step == 0)
    def _():
        sum_proj[...] = jnp.zeros_like(sum_proj)
        sum_expand[...] = jnp.zeros_like(sum_expand)
        sum_reduce[...] = jnp.zeros_like(sum_reduce)
        grad_ebias[...] = jnp.zeros_like(grad_ebias)
        grad_vecs[...] = jnp.zeros_like(grad_vecs)

    mixed_rows = mixed[...]
    cot = cotangent[...]
    middle = tokens[...].astype(F32) + dot(mixed_rows, proj[...]) + vecs[4:5, :]
    xhat, scale = normalise(middle)
    normed = (xhat * vecs[5:6, :] + vecs[6:7, :]).astype(BF16)
    normed_t = normed.T
    branch = None
    grad_normed = None
    for start in range(0, hidden, part):
        cols = pl.ds(start, part)
        into = expand[:, cols]
        back = reduce[cols, :]
        preact = dot(normed, into) + ebias[:, cols]
        cdf, slope = gauss(preact)
        activated = (preact * cdf).astype(BF16)
        grad_preact = (dot_nt(cot, back) * (cdf + slope)).astype(BF16)
        term = dot(activated, back)
        branch = term if branch is None else branch + term
        term = dot_nt(grad_preact, into)
        grad_normed = term if grad_normed is None else grad_normed + term
        sum_reduce[cols, :] += dot_tn(activated, cot)
        sum_expand[:, cols] += dot(normed_t, grad_preact)
        grad_ebias[:, cols] += jnp.sum(grad_preact.astype(F32), axis=0, keepdims=True)
    output[...] = (middle + branch + vecs[7:8, :]).astype(BF16)
    cot32 = cot.astype(F32)
    grads = cot32 + norm_back(grad_normed, vecs[5:6, :], xhat, scale)
    attended = grads.astype(BF16)
    grad_middle[...] = attended
    grad_mixed[...] = dot_nt(attended, proj[...]).astype(BF16)
    sum_proj[...] += dot_tn(mixed_rows, attended)
    grad_vecs[0:1, :] += jnp.sum(attended.astype(F32), axis=0, keepdims=True)
    grad_vecs[1:2, :] += jnp.sum(grad_normed * xhat, axis=0, keepdims=True)
    grad_vecs[2:3, :] += jnp.sum(grad_normed, axis=0, keepdims=True)
    grad_vecs[3:4, :] += jnp.sum(cot32, axis=0, keepdims=True)

    @pl.when(step == pl.num_programs(0) - 1)
    def _():
        grad_proj[...] = sum_proj[...].astype(BF16)
        grad_expand[...] = sum_expand[...].astype(BF16)
        grad_reduce[...] = sum_reduce[...].astype(BF16)


def middle_all(tokens, mixed, cotangent, vecs, ebias, proj, expand, reduce, block=512, part=512):
    rows, width = tokens.shape
    row_block = pl.BlockSpec((block, width), lambda i: (i, 0))
    row_shape = jax.ShapeDtypeStruct((rows, width), BF16)
    return pl.pallas_call(
        functools.partial(middle_kernel, part),
        grid=(rows // block,),
        in_specs=[
            row_block,
            row_block,
            row_block,
            resident(vecs.shape),
            resident(ebias.shape),
            resident(proj.shape),
            resident(expand.shape),
            resident(reduce.shape),
        ],
        out_specs=[
            row_block,
            row_block,
            row_block,
            resident(proj.shape),
            resident(expand.shape),
            resident(reduce.shape),
            resident(ebias.shape),
            resident((8, width)),
        ],
        out_shape=[
            row_shape,
            row_shape,
            row_shape,
            jax.ShapeDtypeStruct(proj.shape, BF16),
            jax.ShapeDtypeStruct(expand.shape, BF16),
            jax.ShapeDtypeStruct(reduce.shape, BF16),
            jax.ShapeDtypeStruct(ebias.shape, F32),
            jax.ShapeDtypeStruct((8, width), F32),
        ],
        scratch_shapes=[
            pltpu.VMEM(proj.shape, F32),
            pltpu.VMEM(expand.shape, F32),
            pltpu.VMEM(reduce.shape, F32),
        ],
        compiler_params=params(63),
    )(tokens, mixed, cotangent, vecs, ebias, proj, expand, reduce)


def weight_kernel(normed, dq, dk, dv, grad_weight, grad_vecs, total):
    step = pl.program_id(0)
    width = normed.shape[1]

    @pl.when(step == 0)
    def _():
        total[...] = jnp.zeros_like(total)
        grad_vecs[...] = jnp.zeros_like(grad_vecs)

    rows_t = normed[...].T
    for index, part in enumerate((dq, dk, dv)):
        total[:, index * width : (index + 1) * width] += dot(rows_t, part[...])
    grad_vecs[0:1, :] += jnp.sum(dq[...].astype(F32), axis=0, keepdims=True)
    grad_vecs[1:2, :] += jnp.sum(dv[...].astype(F32), axis=0, keepdims=True)

    @pl.when(step == pl.num_programs(0) - 1)
    def _():
        grad_weight[...] = total[...].astype(BF16)


def qkv_weight_grad(normed, dq, dk, dv, block=512):
    rows, width = normed.shape
    row_block = pl.BlockSpec((block, width), lambda i: (i, 0))
    return pl.pallas_call(
        weight_kernel,
        grid=(rows // block,),
        in_specs=[row_block] * 4,
        out_specs=[resident((width, 3 * width)), resident((8, width))],
        out_shape=[
            jax.ShapeDtypeStruct((width, 3 * width), BF16),
            jax.ShapeDtypeStruct((8, width), F32),
        ],
        scratch_shapes=[pltpu.VMEM((width, 3 * width), F32)],
        compiler_params=params(40),
    )(normed, dq, dk, dv)


def input_kernel(tokens, grad_middle, dq, dk, dv, vecs, weight, input_grad, grad_vecs):
    step = pl.program_id(0)
    width = tokens.shape[1]

    @pl.when(step == 0)
    def _():
        grad_vecs[...] = jnp.zeros_like(grad_vecs)

    xhat, scale = normalise(tokens[...].astype(F32))
    upstream = (
        dot_nt(dq[...], weight[:, :width])
        + dot_nt(dk[...], weight[:, width : 2 * width])
        + dot_nt(dv[...], weight[:, 2 * width :])
    )
    grads = norm_back(upstream, vecs[0:1, :], xhat, scale)
    input_grad[...] = (grad_middle[...].astype(F32) + grads).astype(BF16)
    grad_vecs[0:1, :] += jnp.sum(upstream * xhat, axis=0, keepdims=True)
    grad_vecs[1:2, :] += jnp.sum(upstream, axis=0, keepdims=True)


def input_backward(tokens, grad_middle, dq, dk, dv, vecs, weight, block=512):
    rows, width = tokens.shape
    row_block = pl.BlockSpec((block, width), lambda i: (i, 0))
    return pl.pallas_call(
        input_kernel,
        grid=(rows // block,),
        in_specs=[row_block] * 5 + [resident(vecs.shape), resident(weight.shape)],
        out_specs=[row_block, resident((8, width))],
        out_shape=[
            jax.ShapeDtypeStruct((rows, width), BF16),
            jax.ShapeDtypeStruct((8, width), F32),
        ],
        compiler_params=params(40),
    )(tokens, grad_middle, dq, dk, dv, vecs, weight)


def local(
    tokens,
    segment_ids,
    valid_mask,
    cotangent,
    norm1_gain,
    norm1_bias,
    qkv_weight,
    query_bias,
    value_bias,
    proj_weight,
    proj_bias,
    norm2_gain,
    norm2_bias,
    expand_weight,
    expand_bias,
    reduce_weight,
    reduce_bias,
):
    seq_len = segment_ids.shape[1]
    own = norm1_gain.shape[0]
    per = expand_bias.shape[0] // own
    small = jnp.stack(
        [
            norm1_gain,
            norm1_bias,
            query_bias,
            value_bias,
            proj_bias,
            norm2_gain,
            norm2_bias,
            reduce_bias,
            *jnp.split(expand_bias, per),
        ]
    )
    small = lax.all_gather(small, "fsdp", axis=0)
    shards = small.shape[0]
    vecs = small[:, :8].swapaxes(0, 1).reshape(8, shards * own).astype(F32)
    ebias = small[:, 8:].reshape(1, shards * own * per).astype(F32)
    qkv_full = lax.all_gather(qkv_weight, "fsdp", axis=0, tiled=True)
    proj_full = lax.all_gather(proj_weight, "fsdp", axis=0, tiled=True)
    expand_full = lax.all_gather(expand_weight, "fsdp", axis=0, tiled=True)
    reduce_full = lax.all_gather(reduce_weight, "fsdp", axis=0, tiled=True)

    table = clip_table(segment_ids, valid_mask)
    qkv, normed1 = qkv_forward(tokens, vecs, qkv_full)
    mixed, inverse, exps = attend_forward(table, qkv, seq_len)
    (
        output,
        grad_middle,
        grad_mixed,
        grad_proj,
        grad_expand,
        grad_reduce,
        grad_ebias,
        middle_vecs,
    ) = middle_all(tokens, mixed, cotangent, vecs, ebias, proj_full, expand_full, reduce_full)

    def shard(grad):
        part = lax.psum_scatter(grad, "fsdp", scatter_dimension=0, tiled=True)
        return lax.psum(part, "rep").astype(F32)

    sum_reduce = shard(grad_reduce)
    sum_expand = shard(grad_expand)
    sum_proj = shard(grad_proj)
    dq, dk, dv = attend_backward(table, qkv, grad_mixed, mixed, inverse, exps, seq_len)
    grad_qkv, qkv_vecs = qkv_weight_grad(normed1, dq, dk, dv)
    sum_qkv = shard(grad_qkv)
    input_grad, input_vecs = input_backward(tokens, grad_middle, dq, dk, dv, vecs, qkv_full)

    vec_rows = jnp.concatenate([input_vecs[:2], qkv_vecs[:2], middle_vecs[:4]], axis=0)
    vec_rows = vec_rows.reshape(8, shards, own).swapaxes(0, 1)
    bias_rows = grad_ebias.reshape(shards, per, own)
    small_grads = jnp.concatenate([vec_rows, bias_rows], axis=1)
    small_grads = lax.psum(small_grads, "rep")
    small_grads = lax.psum_scatter(small_grads, "fsdp", scatter_dimension=0)
    return (
        output,
        input_grad,
        small_grads[0],
        small_grads[1],
        sum_qkv,
        small_grads[2],
        small_grads[3],
        sum_proj,
        small_grads[4],
        small_grads[5],
        small_grads[6],
        sum_expand,
        small_grads[8:].reshape(-1),
        sum_reduce,
        small_grads[7],
    )


def solution(mesh):
    rows = P(("rep", "fsdp"), None)
    vector = P("fsdp")
    matrix = P("fsdp", None)
    params_specs = (
        vector,
        vector,
        matrix,
        vector,
        vector,
        matrix,
        vector,
        vector,
        vector,
        matrix,
        vector,
        matrix,
        vector,
    )
    return jax.shard_map(
        local,
        mesh=mesh,
        in_specs=(rows, rows, rows, rows) + params_specs,
        out_specs=(rows, rows) + params_specs,
        check_vma=False,
    )
```

time: 1100 us -> 634 us (0.58)
  matrix products: 554 us -> 0 us
  waiting for transfers between devices: 77.3 us -> 324 us
  Pallas kernels: 0 us -> 227 us
  other arithmetic: 193 us -> 9.34 us
  local copies, waits for them, and re-layouts: 143 us -> 23.9 us
  blocking collectives: 83.1 us -> 26 us
  loops' own time: 31.3 us -> 0 us
    dot_general x40 -> x0, matrix products: 554 us -> none  [the longest x8 112 us: block_scores(): jnp.einsum('qhd,khd->hqk', query_rows, key_heads, preferred_element_type=...]
    pallas_call x0 -> x6, Pallas kernels: none -> 227 us  [the longest x1 103 us: middle_all(): pl.pallas_call(functools.partial(middle_kernel, part), grid=(rows // bloc...]
    convert_element_type x27 -> x6, other arithmetic: 114 us -> 6.1 us  [the longest x4 6.1 us: shard(): return lax.psum(part, 'rep').astype(F32)]
    all_gather x4, waiting for transfers between devices: 0.01 us -> 104 us  [the longest x1 52 us: local(): reduce_full = lax.all_gather(reduce_weight, 'fsdp', axis=0, tiled=True)]
    reduce_scatter x4 -> x5, waiting for transfers between devices: 57.1 us -> 161 us  [the longest x4 130 us: shard(): part = lax.psum_scatter(grad, 'fsdp', scatter_dimension=0, tiled=True)]
    reduce_sum x13 -> x1, other arithmetic: 72.7 us -> 1.09 us  [clip_table(): jnp.sum(((segments == clips) & (valid_mask[:, None, :] == 1)).astype(jnp....]
    unnamed x2 -> x0, blocking collectives: 60.5 us -> none
    while x64 -> x0, local copies, waits for them, and re-layouts: 42 us -> none  [the longest x4 18.4 us: local(): lax.map(attend_back, (split_heads(queries), split_heads(key_rows), split_...]
  transfers between devices with their start and end apart: 9 -> 10, of which waited for: 3 -> 8; matrix products, arithmetic and copies ran while one was open for 73% -> 1% of each run, Pallas kernels for 0% -> 20%
where the time goes in v1:
time: 634 us; the launch traced here: 625 us
  waiting for transfers between devices  324 us (51%)
  Pallas kernels  227 us (36%)
  blocking collectives  26 us (4%)
  local copies, waits for them, and re-layouts  23.9 us (4%)
  between operations  14.5 us (2%)
  other arithmetic  9.34 us (1%)
    reduce_scatter x4, waiting for transfers between devices, shard(): part = lax.psum_scatter(grad, 'fsdp', scatter_dimension=0, tiled=True)  130 us
    pallas_call x1, Pallas kernels, middle_all(): pl.pallas_call(functools.partial(middle_kernel, part), grid=(rows // bloc...  103 us
    pallas_call x1, Pallas kernels, attend_backward(): pl.pallas_call(functools.partial(back_kernel, pairs), grid_spec=pltpu.Pre...  57.4 us
    psum x1, waiting for transfers between devices, shard(): return lax.psum(part, 'rep').astype(F32)  54.8 us
    all_gather x1, waiting for transfers between devices, local(): reduce_full = lax.all_gather(reduce_weight, 'fsdp', axis=0, tiled=True)  52 us
    reduce_scatter x1, waiting for transfers between devices, local(): small_grads = lax.psum_scatter(small_grads, 'fsdp', scatter_dimension=0)  31.3 us
    pallas_call x1, Pallas kernels, attend_forward(): pl.pallas_call(functools.partial(attend_kernel, pairs), grid_spec=pltpu.P...  29.6 us
    all_gather x1, waiting for transfers between devices, local(): expand_full = lax.all_gather(expand_weight, 'fsdp', axis=0, tiled=True)  28.6 us
  transfers between devices with their start and end apart: 10, of which 8 were waited for; matrix products, arithmetic and copies ran while one was open for 1% of the time, Pallas kernels for 20%

profile of v1, /device:TPU:0, one launch (start us, length us, event | category | flops | bytes accessed | tf_op | source)
XLA Modules:
  0.0 624.9 jit_solution(10054562882986003588)
XLA Ops:
  7.2 0.7 all-gather.7.cloned.1.call-update
  8.0 0.7 all-gather.9.cloned.1.call-update
  8.7 0.7 all-gather.11.cloned.1.call-update
  9.4 0.5 all-gather.13.cloned.1.call-update
  10.0 0.7 broadcast_compare_fusion
  10.7 1.1 fusion.2
  11.8 0.1 copy.41
  12.2 0.1 copy.44
  12.4 0.9 slice_bitcast_fusion.8
  13.3 0.8 stack.60
  14.1 15.8 %all-gather.1 = bf16[8,12,96]{2,1,0:T(8,128)(2,1)S(1)} all-gather(bf16[1,12,96]{2,1,0:T(8,128)(2,1)S(1)} %bitcast.94), channel_id=2, replica_groups=mesh['rep'=4,'fsdp'=8] {'fsdp'}, dimensions={0}, use_global_device_ids=true | all-gather | bytes 20736 | tf_op jit(solution)/shard_map/all_gather | solution.py:656
  30.0 0.7 reshape.226.ebias
  30.7 23.3 %all-gather.7.cloned.1.call-done.weight = bf16[768,2304]{1,0:T(8,128)(2,1)} async-done(((bf16[96,2304]{1,0:T(8,128)(2,1)}), bf16[768,2304]{1,0:T(8,128)(2,1)}) %all-gather.7.cloned.1.call-update) | async-done | bytes 3538960 | tf_op jit(solution)/shard_map/all_gather | solution.py:660
  54.1 1.9 copy-done
  56.0 2.0 copy-done.2
  58.0 10.9 %shard_map.280 = (bf16[2048,2304]{1,0:T(8,128)(2,1)}, bf16[2048,768]{1,0:T(8,128)(2,1)S(1)}) custom-call(bf16[2048,768]{1,0:T(8,128)(2,1)S(1)} %copy-done, f32[8,768]{1,0:T(8,128)S(1)} %reshape.225.vecs, bf16[768,2304]{1,0:T(8,128)(2,1)S(1)} %copy-done.2), custom_call_target="tpu_custom_call" | custom-call | tf_op jit(solution)/shard_map/pallas_call | solution.py:73
  68.9 1.7 copy-done.10
  70.5 29.6 %shard_map.281 = (bf16[2048,768]{1,0:T(8,128)(2,1)S(1)}, f32[2048,768]{1,0:T(8,128)}, bf16[2,12,1536,256]{3,2,1,0:T(8,128)(2,1)}) custom-call(s32[60]{0:T(128)S(1)} %reshape.221.table, bf16[2048,2304]{1,0:T(8,128)(2,1)} %get-tuple-element.35.queries.keys.values, bf16[2048,2304]{1,0:T(8,128)(2,1)} %get-tuple-element.35.queries.keys.values, ...), custom_call_target="tpu_custom_call" | custom-call | tf_op jit(solution)/shard_map/pallas_call | solution.py:230
  100.1 1.7 copy-done.3
  101.8 28.6 %all-gather.11.cloned.1.call-done.expand = bf16[768,3072]{1,0:T(8,128)(2,1)} async-done(((bf16[96,3072]{1,0:T(8,128)(2,1)}), bf16[768,3072]{1,0:T(8,128)(2,1)}) %all-gather.11.cloned.1.call-update) | async-done | bytes 4718608 | tf_op jit(solution)/shard_map/all_gather | solution.py:662
  130.4 52.0 %all-gather.13.cloned.1.call-done.reduce = bf16[3072,768]{1,0:T(8,128)(2,1)} async-done(((bf16[384,768]{1,0:T(8,128)(2,1)}), bf16[3072,768]{1,0:T(8,128)(2,1)}) %all-gather.13.cloned.1.call-update) | async-done | bytes 4718608 | tf_op jit(solution)/shard_map/all_gather | solution.py:663
  182.5 103.2 %shard_map.282 = (bf16[2048,768]{1,0:T(8,128)(2,1)}, bf16[2048,768]{1,0:T(8,128)(2,1)}, bf16[2048,768]{1,0:T(8,128)(2,1)}, bf16[768,768]{1,0:T(8,128)(2,1)}, bf1...) custom-call(bf16[2048,768]{1,0:T(8,128)(2,1)} %tokens.5, ...), custom_call_target="tpu_custom_call" | custom-call | tf_op jit(solution)/shard_map/pallas_call | solution.py:506
  285.8 57.4 %shard_map.283 = (bf16[2048,768]{1,0:T(8,128)(2,1)S(1)}, bf16[2048,768]{1,0:T(8,128)(2,1)}, bf16[2048,768]{1,0:T(8,128)(2,1)}) custom-call(s32[60]{0:T(128)S(1)} %reshape.221.table, bf16[2048,2304]{1,0:T(8,128)(2,1)} %get-tuple-element.35.queries.keys.values, bf16[2048,2304]{1,0:T(8,128)(2,1)} %get-tuple-element.35.queries.keys.values, ...), custom_call_target="tpu_custom_call" | custom-call | tf_op jit(solution)/shard_map/pallas_call | solution.py:389
  343.3 3.0 copy-done.6
  346.3 1.9 copy-done.8
  348.2 11.6 %shard_map.285 = (bf16[768,2304]{1,0:T(8,128)(2,1)}, f32[8,768]{1,0:T(8,128)S(1)}) custom-call(bf16[2048,768]{1,0:T(8,128)(2,1)S(1)} %copy-done.11, bf16[2048,768]{1,0:T(8,128)(2,1)S(1)} %get-tuple-element.42.dq, bf16[2048,768]{1,0:T(8,128)(2,1)S(1)} %copy-done.6, bf16[2048,768]{1,0:T(8,128)(2,1)S(1)} %copy-done.8), custom_call_target="tpu_custom_call" | custom-call | tf_op jit(solution)/shard_map/pallas_call | solution.py:571
  359.8 0.7 reduce-scatter.10.cloned.1.call-update
  360.6 0.7 reduce-scatter.12.cloned.1.call-update
  361.3 1.1 copy-done.1
  362.4 1.9 copy-done.5
  364.3 2.0 copy-done.7
  366.3 1.9 copy-done.9
  368.2 14.3 %shard_map.284 = (bf16[2048,768]{1,0:T(8,128)(2,1)}, f32[8,768]{1,0:T(8,128)S(1)}) custom-call(bf16[2048,768]{1,0:T(8,128)(2,1)S(1)} %copy-done.1, bf16[2048,768]{1,0:T(8,128)(2,1)S(1)} %copy-done.9, bf16[2048,768]{1,0:T(8,128)(2,1)S(1)} %copy-done.5, bf16[2048,768]{1,0:T(8,128)(2,1)S(1)} %copy-done.7, bf16[2048,768]{1,0:T(8,128)(2,1)} %get-tuple-element.44.dv, ...), custom_call_target="tpu_custom_call" | custom-call | tf_op jit(solution)/shard_map/pallas_call | solution.py:608
  382.6 0.5 broadcast.434
  383.1 0.7 reduce.3
  383.9 0.6 pad_maximum_fusion
  384.7 17.9 %reduce-scatter.6.cloned.1.call-done = bf16[96,2304]{1,0:T(8,128)(2,1)} async-done(((bf16[768,2304]{1,0:T(8,128)(2,1)}), bf16[96,2304]{1,0:T(8,128)(2,1)}) %reduce-scatter.6.cloned.1.call-update) | async-done | bytes 442384 | tf_op jit(solution)/shard_map/reduce_scatter | solution.py:680
  402.6 55.9 %reduce-scatter.10.cloned.1.call-done = bf16[96,3072]{1,0:T(8,128)(2,1)} async-done(((bf16[768,3072]{1,0:T(8,128)(2,1)}), bf16[96,3072]{1,0:T(8,128)(2,1)}) %reduce-scatter.10.cloned.1.call-update) | async-done | bytes 589840 | tf_op jit(solution)/shard_map/reduce_scatter | solution.py:680
  458.5 55.8 %reduce-scatter.12.cloned.1.call-done = bf16[384,768]{1,0:T(8,128)(2,1)} async-done(((bf16[3072,768]{1,0:T(8,128)(2,1)}), bf16[384,768]{1,0:T(8,128)(2,1)}) %reduce-scatter.12.cloned.1.call-update) | async-done | bytes 589840 | tf_op jit(solution)/shard_map/reduce_scatter | solution.py:680
  514.3 31.3 %reduce-scatter.14.cloned.1.call-done = f32[1,12,96]{2,1,0:T(8,128)} async-done(((f32[8,12,96]{2,1,0:T(8,128)}), f32[1,12,96]{2,1,0:T(8,128)}) %reduce-scatter.14.cloned.1.call-update) | async-done | bytes 4624 | tf_op jit(solution)/shard_map/reduce_scatter | solution.py:696
  545.5 10.2 %psum.40 = f32[1,12,96]{2,1,0:T(8,128)S(1)} all-reduce(f32[1,12,96]{2,1,0:T(8,128)} %reduce-scatter.14.cloned.1.call-done), channel_id=1, replica_groups=mesh['rep'=4,'fsdp'=8] {'rep'}, use_global_device_ids=true, to_apply=%region_3.4 | all-reduce | flops 1152 | bytes 9216 | tf_op jit(solution)/shard_map/psum | solution.py:695
  555.7 0.7 reshape.224
  556.4 0.5 slice_bitcast_fusion
  556.9 54.8 %all-reduce.3.cloned.1.call-done = (bf16[96,2304]{1,0:T(8,128)(2,1)}, bf16[96,768]{1,0:T(8,128)(2,1)}, bf16[96,3072]{1,0:T(8,128)(2,1)}, bf16[384,768]{1,0:T(8,128)(2,1)}) async-done(((bf16[96,2304]{1,0:T(8,128)(2,1)}, bf16[96,768]{1,0:T(8,128)(2,1)}, bf16[96,3072]{1,0:T(8,128)(2,1)}, bf16[384,768]{1,0:T(8,128)(2,1)}), (bf16[96,2304]{1,0:T(8,128)(2,1)}, bf16[96,768]{1,0:T(8,128)(2,1)}, ...) | async-done | bytes 1769488 | tf_op jit(solution)/shard_map/psum | solution.py:681
  611.8 2.2 convert_element_type.97
  614.0 2.2 convert_element_type.98
  616.2 1.0 convert_element_type.95
  617.1 0.7 convert_element_type.96
  (62 shorter events, 1.2 us)
Async XLA Ops:
  7.2 46.9 %all-gather.7.cloned.1.call-start = ((), (), s32[]{:S(2)}) async-start(), calls=%async_computation.5 | async-start | bytes 3981312 | tf_op jit(solution)/shard_map/all_gather | solution.py:660
  7.9 93.9 %all-gather.9.cloned.1.call-start = ((), (), s32[]{:S(2)}) async-start(), calls=%async_computation.6 | async-start | bytes 1327104 | tf_op jit(solution)/shard_map/all_gather | solution.py:661
  8.7 121.8 %all-gather.11.cloned.1.call-start = ((), (), s32[]{:S(2)}) async-start(), calls=%async_computation.7 | async-start | bytes 5308416 | tf_op jit(solution)/shard_map/all_gather | solution.py:662
  9.4 173.1 %all-gather.13.cloned.1.call-start = ((), (), s32[]{:S(2)}) async-start(), calls=%async_computation.8 | async-start | bytes 5308416 | tf_op jit(solution)/shard_map/all_gather | solution.py:663
  10.0 374.7 %reduce-scatter.8.cloned.1.call-start = ((), (), s32[]{:S(2)}) async-start(), calls=%async_computation.10 | async-start | bytes 1327104 | tf_op jit(solution)/shard_map/reduce_scatter | solution.py:680
  30.0 38.9 %copy-start.12 = (f32[8,768]{1,0:T(8,128)}, f32[8,768]{1,0:T(8,128)S(1)}, u32[]{:S(2)}) copy-start(f32[8,768]{1,0:T(8,128)S(1)} %reshape.225.vecs) | copy-start | bytes 73732
  54.1 1.9 copy-start
  55.9 2.0 copy-start.2
  68.9 1.7 copy-start.10
  100.1 1.7 copy-start.3
  285.8 116.8 %reduce-scatter.6.cloned.1.call-start = ((), (), s32[]{:S(2)}) async-start(), calls=%async_computation.9 | async-start | bytes 3981312 | tf_op jit(solution)/shard_map/reduce_scatter | solution.py:680
  285.8 57.4 %copy-start.11 = (bf16[2048,768]{1,0:T(8,128)(2,1)S(1)}, bf16[2048,768]{1,0:T(8,128)(2,1)}, u32[]{:S(2)}) copy-start(bf16[2048,768]{1,0:T(8,128)(2,1)} %copy-done.10) | copy-start | bytes 9437188
  343.2 16.5 %copy-start.4 = (bf16[2048,768]{1,0:T(8,128)(2,1)}, bf16[2048,768]{1,0:T(8,128)(2,1)S(1)}, u32[]{:S(2)}) copy-start(bf16[2048,768]{1,0:T(8,128)(2,1)S(1)} %get-tuple-element.42.dq) | copy-start | bytes 9437188
  343.2 3.0 copy-start.6
  346.3 1.9 copy-start.8
  359.7 98.7 %reduce-scatter.10.cloned.1.call-start = ((), (), s32[]{:S(2)}) async-start(), calls=%async_computation.11 | async-start | bytes 5308416 | tf_op jit(solution)/shard_map/reduce_scatter | solution.py:680
  360.5 1.9 copy-start.1
  360.5 1.9 copy-start.13
  360.5 153.7 %reduce-scatter.12.cloned.1.call-start = ((), (), s32[]{:S(2)}) async-start(), calls=%async_computation.12 | async-start | bytes 5308416 | tf_op jit(solution)/shard_map/reduce_scatter | solution.py:680
  361.3 184.3 %reduce-scatter.14.cloned.1.call-start = ((), (), s32[]{:S(2)}) async-start(), calls=%async_computation.13 | async-start | bytes 73728 | tf_op jit(solution)/shard_map/reduce_scatter | solution.py:696
  362.4 1.9 copy-start.5
  364.3 2.0 copy-start.7
  366.3 1.9 copy-start.9
  368.2 14.3 %copy-start.17 = (f32[8,768]{1,0:T(8,128)S(1)}, f32[8,768]{1,0:T(8,128)}, u32[]{:S(2)}) copy-start(f32[8,768]{1,0:T(8,128)} %get-tuple-element.49) | copy-start | bytes 73732
  368.2 15.0 %copy-start.16 = (f32[1,3072]{1,0:T(1,128)S(1)}, f32[1,3072]{1,0:T(1,128)}, u32[]{:S(2)}) copy-start(f32[1,3072]{1,0:T(1,128)} %get-tuple-element.50) | copy-start | bytes 36868
  384.6 227.2 %all-reduce.3.cloned.1.call-start = ((), (), s32[]{:S(2)}) async-start(), calls=%async_computation.14 | async-start | bytes 3538944 | tf_op jit(solution)/shard_map/psum | solution.py:681
  611.8 4.4 copy-start.14
  611.8 5.4 copy-start.15
Sparse Core Ops, SparseCore 0:
  9.7 44.3 all-gather.6
  55.7 21.5 all-gather.8
  78.9 51.4 all-gather.10
  131.9 50.5 all-gather.12
  285.9 31.6 reduce-scatter.7
  359.9 42.6 reduce-scatter.5
  405.0 53.4 reduce-scatter.9
  460.9 53.3 reduce-scatter.11
  517.1 28.3 reduce-scatter.13
  548.8 62.8 all-reduce.2

commit v2 on v1

--- a/solution.py
+++ b/solution.py
@@ -1,4 +1,5 @@
 import functools
+import math
 
 import jax
 import jax.numpy as jnp
@@ -56,11 +57,309 @@
     return scale * (weighted - first - xhat * second)
 
 
-def qkv_kernel(tokens, vecs, weight, qkv, normed):
+def core_swap(value):
+    count = lax.axis_size("fsdp")
+    return lax.ppermute(value, "fsdp", [(i, i ^ 1) for i in range(count)])
+
+
+def chip_shift(value, hops):
+    count = lax.axis_size("fsdp")
+    return lax.ppermute(value, "fsdp", [(i, (i + 2 * hops) % count) for i in range(count)])
+
+
+def replica_swap(value, bits):
+    return lax.ppermute(value, "rep", [(i, i ^ bits) for i in range(4)])
+
+
+def place_table():
+    shard = lax.axis_index("fsdp")
+    replica = lax.axis_index("rep")
+    return jnp.stack([shard // 2, shard % 2, replica // 2, replica % 2]).astype(jnp.int32)
+
+
+def gather_pieces(piece, split):
+    chips = lax.axis_size("fsdp") // 2
+    along = jnp.concatenate([chip_shift(piece, hop) for hop in range(1, chips)], axis=0)
+    from_x = replica_swap(along, 1)
+    from_y = replica_swap(along, 2)
+    low = replica_swap(from_x[:, :split], 2)
+    high = replica_swap(from_y[:, split:], 1)
+    here = (along, from_x, from_y, low, high)
+    return here, tuple(core_swap(part) for part in here)
+
+
+def fetch_copies(place, targets, owns, pieces, split, chips, sems):
+    chip, core, row_bit, col_bit = (place[i] for i in range(4))
+    count = 0
+    made = []
+
+    def add(source, target):
+        nonlocal count
+        made.append(pltpu.make_async_copy(source, target, sems.at[count]))
+        count += 1
+
+    for other in range(2):
+        side = core ^ other
+        along, from_x, from_y, low, high = pieces[other]
+        height = along.shape[0] // (chips - 1)
+        step = math.gcd(height, 16)
+        for number, (target, stacked, column) in enumerate(targets):
+            rows = target.shape[0] // (2 * chips)
+            start = pl.multiple_of((2 * chip + side) * rows, step)
+            add(owns[other][number], target.at[pl.ds(start, rows), :])
+            for hop in range(1, chips):
+                shard = 2 * lax.rem(chip - hop + chips, chips) + side
+                source_rows = pl.ds((hop - 1) * height, height)
+                for flip in range(4):
+                    across = row_bit ^ (flip // 2)
+                    aside = col_bit ^ (flip % 2)
+                    if stacked:
+                        width = target.shape[1]
+                        spans = []
+                        for half in range(rows // (4 * height)):
+                            at = shard * rows + (across * 2 + aside) * (rows // 4) + half * height
+                            spans.append((column + half * width, width, at, 0))
+                    else:
+                        width = target.shape[1] // 2
+                        spans = [(column, width, shard * rows + across * height, aside * width)]
+                    for first, size, row, col in spans:
+                        row = pl.multiple_of(row, step)
+                        cuts = [(first, size, 0)]
+                        if flip == 3 and first < split < first + size:
+                            cuts = [
+                                (first, split - first, 0),
+                                (split, first + size - split, split - first),
+                            ]
+                        for begin, length, extra in cuts:
+                            origin = (along, from_x, from_y, low)[flip]
+                            if flip == 3 and begin >= split:
+                                origin = high
+                                begin = begin - split
+                            to = col if isinstance(col, int) else pl.multiple_of(col + extra, 128)
+                            add(
+                                origin.at[source_rows, pl.ds(begin, length)],
+                                target.at[pl.ds(row, height), pl.ds(to, length)],
+                            )
+    return made
+
+
+def spread_copies(place, targets, small, blank, mine, theirs, chips, sems):
+    core = place[1]
+    count = 0
+    made = []
+    height = mine.shape[0] // (4 * chips)
+    step = math.gcd(height, 16)
+    for other, packed in ((1, theirs), (0, mine)):
+        side = core ^ other
+        for chip in range(chips):
+            shard = 2 * chip + side
+            for quarter in range(4):
+                out_rows = pl.ds((chip * 4 + quarter) * height, height)
+                moves = []
+                column = 0
+                for target, stacked in targets:
+                    rows = target.shape[0] // (2 * chips)
+                    if stacked:
+                        width = target.shape[1]
+                        for half in range(rows // (4 * height)):
+                            row = shard * rows + quarter * (rows // 4) + half * height
+                            row = pl.multiple_of(row, step)
+                            moves.append((target.at[pl.ds(row, height), :], column, width))
+                            column += width
+                    else:
+                        width = target.shape[1] // 2
+                        row = pl.multiple_of(shard * rows + (quarter // 2) * height, step)
+                        cols = pl.ds((quarter % 2) * width, width)
+                        moves.append((target.at[pl.ds(row, height), cols], column, width))
+                        column += width
+                if quarter == 0:
+                    moves.append((small.at[shard], column, 128))
+                else:
+                    moves.append((blank.at[...], column, 128))
+                for source, column, width in moves:
+                    made.append(
+                        pltpu.make_async_copy(
+                            source, packed.at[out_rows, pl.ds(column, width)], sems.at[count]
+                        )
+                    )
+                    count += 1
+    return made
+
+
+def run_copies(made):
+    for copy in made:
+        copy.start()
+    for copy in made:
+        copy.wait()
+
+
+def add16(left, right):
+    return left.astype(F32) + right.astype(F32)
+
+
+def first_sum(height, place, mine, other, keep_a, send_a, keep_b, send_b):
+    row_bit, col_bit = place[2], place[3]
+    cut = keep_a.shape[1]
+    step = math.gcd(height, 16)
+
+    def piece(quarter, cols):
+        rows = pl.ds(pl.multiple_of(quarter * height, step), height)
+        return add16(mine[rows, cols], other[rows, cols]).astype(BF16)
+
+    for bit in range(2):
+        out = pl.ds(bit * height, height)
+        keep_a[out, :] = piece(bit * 2 + col_bit, pl.ds(0, cut))
+        send_a[out, :] = piece(bit * 2 + 1 - col_bit, pl.ds(0, cut))
+        keep_b[out, :] = piece(row_bit * 2 + bit, pl.ds(cut, mine.shape[1] - cut))
+        send_b[out, :] = piece((1 - row_bit) * 2 + bit, pl.ds(cut, mine.shape[1] - cut))
+
+
+def second_sum(height, place, keep_a, got_a, keep_b, got_b, next_a, send_a, next_b, send_b):
+    step = math.gcd(height, 16)
+    for bit, keep, got, stay, send in (
+        (place[2], keep_a, got_a, next_a, send_a),
+        (place[3], keep_b, got_b, next_b, send_b),
+    ):
+        for which, out in ((bit, stay), (1 - bit, send)):
+            rows = pl.ds(pl.multiple_of(which * height, step), height)
+            out[...] = add16(keep[rows, :], got[rows, :]).astype(BF16)
+
+
+def third_sum(height, place, keep_a, got_a, keep_b, got_b, own, *sends):
+    chips = len(sends) + 1
+    cut = keep_a.shape[1]
+    step = math.gcd(height, 16)
+    for hop, out in enumerate((own, *sends)):
+        at = lax.rem(place[0] + hop, chips)
+        rows = pl.ds(pl.multiple_of(at * height, step), height)
+        out[:, :cut] = add16(keep_a[rows, :], got_a[rows, :]).astype(out.dtype)
+        out[:, cut:] = add16(keep_b[rows, :], got_b[rows, :]).astype(out.dtype)
+
+
+def fourth_sum(own, *refs):
+    total = own[...]
+    for ref in refs[:-1]:
+        total = total + ref[...].astype(F32)
+    refs[-1][...] = total.astype(BF16)
+
+
+def last_spread(stacks, place, own, from_x, from_y, from_xy, *outs):
+    replica = place[2] * 2 + place[3]
+    height, packed = own.shape
+    step = math.gcd(height, 16)
+    for flip, source in enumerate((own, from_x, from_y, from_xy)):
+        across = place[2] ^ (flip // 2)
+        aside = place[3] ^ (flip % 2)
+        column = 0
+        for stacked, out in zip(stacks, outs):
+            rows, width = out.shape
+            if stacked:
+                for half in range(rows // (4 * height)):
+                    at = (across * 2 + aside) * (rows // 4) + half * height
+                    out[pl.ds(pl.multiple_of(at, step), height), :] = source[
+                        :, column : column + width
+                    ].astype(F32)
+                    column += width
+            else:
+                width = width // 2
+                at = pl.ds(pl.multiple_of(across * height, step), height)
+                cols = pl.ds(pl.multiple_of(aside * width, 128), width)
+                out[at, cols] = source[:, column : column + width].astype(F32)
+                column += width
+
+        @pl.when((replica ^ flip) == 0)
+        def _():
+            outs[-1][...] = source[0:16, packed - 128 :].astype(F32)
+
+
+def small_call(body, place, inputs, shapes, grid=None, in_specs=None, out_specs=None):
+    if grid is None:
+        grid = (1,)
+        in_specs = [pl.BlockSpec(value.shape, lambda i, t: (0, 0)) for value in inputs]
+        out_specs = [pl.BlockSpec(shape.shape, lambda i, t: (0, 0)) for shape in shapes]
+    return pl.pallas_call(
+        body,
+        grid_spec=pltpu.PrefetchScalarGridSpec(
+            num_scalar_prefetch=1, grid=grid, in_specs=in_specs, out_specs=out_specs
+        ),
+        out_shape=shapes,
+        compiler_params=params(40),
+    )(place, *inputs)
+
+
+def sum_pieces(place, mine, theirs, cut, stacks, out_shapes):
+    chips = lax.axis_size("fsdp") // 2
+    height = mine.shape[0] // (4 * chips)
+    packed = mine.shape[1]
+    other = core_swap(theirs)
+
+    def shape(rows, cols, dtype=BF16):
+        return jax.ShapeDtypeStruct((rows, cols), dtype)
+
+    def rows_of(count, cols):
+        return pl.BlockSpec((count * height, cols), lambda i, t: (i, 0))
+
+    keep_a, send_a, keep_b, send_b = small_call(
+        functools.partial(first_sum, height),
+        place,
+        (mine, other),
+        [shape(2 * chips * height, cut)] * 2 + [shape(2 * chips * height, packed - cut)] * 2,
+        (chips,),
+        [rows_of(4, packed)] * 2,
+        [rows_of(2, cut)] * 2 + [rows_of(2, packed - cut)] * 2,
+    )
+    got_a = replica_swap(send_a, 1)
+    got_b = replica_swap(send_b, 2)
+    keep_a, send_a, keep_b, send_b = small_call(
+        functools.partial(second_sum, height),
+        place,
+        (keep_a, got_a, keep_b, got_b),
+        [shape(chips * height, cut)] * 2 + [shape(chips * height, packed - cut)] * 2,
+        (chips,),
+        [rows_of(2, cut)] * 2 + [rows_of(2, packed - cut)] * 2,
+        [rows_of(1, cut)] * 2 + [rows_of(1, packed - cut)] * 2,
+    )
+    got_a = replica_swap(send_a, 2)
+    got_b = replica_swap(send_b, 1)
+    own, *sends = small_call(
+        functools.partial(third_sum, height),
+        place,
+        (keep_a, got_a, keep_b, got_b),
+        [shape(height, packed, F32)] + [shape(height, packed)] * (chips - 1),
+    )
+    got = [chip_shift(send, hop + 1) for hop, send in enumerate(sends)]
+    (total,) = small_call(
+        lambda table, *refs: fourth_sum(*refs), place, (own, *got), [shape(height, packed)]
+    )
+    quarters = (total, replica_swap(total, 1), replica_swap(total, 2), replica_swap(total, 3))
+    return small_call(
+        functools.partial(last_spread, stacks),
+        place,
+        quarters,
+        [jax.ShapeDtypeStruct(s, F32) for s in out_shapes] + [shape(16, 128, F32)],
+    )
+
+
+def small_blocks(rows_of_shard, small, shards, own):
+    small[...] = jnp.zeros_like(small)
+    for shard in range(shards):
+        rows = rows_of_shard(shard)
+        small[shard, 0 : rows.shape[0], 0:own] = rows.astype(BF16)
+
+
+def qkv_kernel(chips, split, place, tokens, vecs, *refs):
+    owns = (refs[0:1], refs[1:2])
+    pieces = (refs[2:7], refs[7:12])
+    qkv, unit, weight, sems = refs[12:]
     width = tokens.shape[1]
+
+    @pl.when(pl.program_id(0) == 0)
+    def _():
+        run_copies(fetch_copies(place, [(weight, False, 0)], owns, pieces, split, chips, sems))
+
     xhat, _ = normalise(tokens[...].astype(F32))
+    unit[...] = xhat.astype(BF16)
     rows = (xhat * vecs[0:1, :] + vecs[1:2, :]).astype(BF16)
-    normed[...] = rows
     query = dot(rows, weight[:, :width]) + vecs[2:3, :]
     qkv[:, :width] = query.astype(BF16) * jnp.asarray(0.125, BF16)
     qkv[:, width : 2 * width] = dot(rows, weight[:, width : 2 * width]).astype(BF16)
@@ -68,26 +367,42 @@
     qkv[:, 2 * width :] = value.astype(BF16)
 
 
-def qkv_forward(tokens, vecs, weight, block=512):
+def hbm():
+    return pl.BlockSpec(memory_space=pl.ANY)
+
+
+def qkv_forward(place, tokens, vecs, own, pieces, split, block=512):
     rows, width = tokens.shape
+    chips = lax.axis_size("fsdp") // 2
+    sources = [own, core_swap(own), *pieces[0], *pieces[1]]
+    zero = lambda i, t: (0, 0)
     return pl.pallas_call(
-        qkv_kernel,
-        grid=(rows // block,),
-        in_specs=[
-            pl.BlockSpec((block, width), lambda i: (i, 0)),
-            resident(vecs.shape),
-            resident(weight.shape),
-        ],
-        out_specs=[
-            pl.BlockSpec((block, 3 * width), lambda i: (i, 0)),
-            pl.BlockSpec((block, width), lambda i: (i, 0)),
-        ],
+        functools.partial(qkv_kernel, chips, split),
+        grid_spec=pltpu.PrefetchScalarGridSpec(
+            num_scalar_prefetch=1,
+            grid=(rows // block,),
+            in_specs=[
+                pl.BlockSpec((block, width), lambda i, t: (i, 0)),
+                pl.BlockSpec(vecs.shape, zero),
+            ]
+            + [hbm()] * len(sources),
+            out_specs=[
+                pl.BlockSpec((block, 3 * width), lambda i, t: (i, 0)),
+                pl.BlockSpec((block, width), lambda i, t: (i, 0)),
+                resident((width, 3 * width)),
+            ],
+            scratch_shapes=[pltpu.SemaphoreType.DMA((2 + 10 * (chips - 1),))],
+        ),
         out_shape=[
             jax.ShapeDtypeStruct((rows, 3 * width), BF16),
             jax.ShapeDtypeStruct((rows, width), BF16),
+            jax.ShapeDtypeStruct((width, 3 * width), BF16),
         ],
         compiler_params=params(40),
-    )(tokens, vecs, weight)
+        cost_estimate=pl.CostEstimate(
+            flops=6 * rows * width * width, bytes_accessed=20_000_000, transcendentals=0
+        ),
+    )(place, tokens, vecs, *sources)
 
 
 def clip_table(segment_ids, valid_mask):
@@ -426,36 +741,58 @@
 
 def middle_kernel(
     part,
+    chips,
+    split,
+    place,
     tokens,
     mixed,
     cotangent,
     vecs,
     ebias,
-    proj,
-    expand,
-    reduce,
-    output,
-    grad_middle,
-    grad_mixed,
-    grad_proj,
-    grad_expand,
-    grad_reduce,
-    grad_ebias,
-    grad_vecs,
-    sum_proj,
-    sum_expand,
-    sum_reduce,
+    *refs,
 ):
+    owns = (refs[0:3], refs[3:6])
+    pieces = (refs[6:11], refs[11:16])
+    (
+        output,
+        grad_middle,
+        grad_mixed,
+        mine,
+        theirs,
+        proj,
+        expand,
+        reduce,
+        sum_proj,
+        sum_expand,
+        sum_reduce,
+        sum_ebias,
+        sum_vecs,
+        small,
+        blank,
+        in_sems,
+        out_sems,
+    ) = refs[16:]
     step = pl.program_id(0)
-    hidden = expand.shape[1]
+    width, hidden = expand.shape
+    own = width // (2 * chips)
 
     @pl.when(step == 0)
     def _():
+        targets = [
+            (proj, False, 0),
+            (expand, False, width // 2),
+            (reduce, True, width // 2 + hidden // 2),
+        ]
+        made = fetch_copies(place, targets, owns, pieces, split, chips, in_sems)
+        for copy in made:
+            copy.start()
         sum_proj[...] = jnp.zeros_like(sum_proj)
         sum_expand[...] = jnp.zeros_like(sum_expand)
         sum_reduce[...] = jnp.zeros_like(sum_reduce)
-        grad_ebias[...] = jnp.zeros_like(grad_ebias)
-        grad_vecs[...] = jnp.zeros_like(grad_vecs)
+        sum_ebias[...] = jnp.zeros_like(sum_ebias)
+        sum_vecs[...] = jnp.zeros_like(sum_vecs)
+        for copy in made:
+            copy.wait()
 
     mixed_rows = mixed[...]
     cot = cotangent[...]
@@ -479,7 +816,7 @@
         grad_normed = term if grad_normed is None else grad_normed + term
         sum_reduce[cols, :] += dot_tn(activated, cot)
         sum_expand[:, cols] += dot(normed_t, grad_preact)
-        grad_ebias[:, cols] += jnp.sum(grad_preact.astype(F32), axis=0, keepdims=True)
+        sum_ebias[:, cols] += jnp.sum(grad_preact.astype(F32), axis=0, keepdims=True)
     output[...] = (middle + branch + vecs[7:8, :]).astype(BF16)
     cot32 = cot.astype(F32)
     grads = cot32 + norm_back(grad_normed, vecs[5:6, :], xhat, scale)
@@ -487,109 +824,172 @@
     grad_middle[...] = attended
     grad_mixed[...] = dot_nt(attended, proj[...]).astype(BF16)
     sum_proj[...] += dot_tn(mixed_rows, attended)
-    grad_vecs[0:1, :] += jnp.sum(attended.astype(F32), axis=0, keepdims=True)
-    grad_vecs[1:2, :] += jnp.sum(grad_normed * xhat, axis=0, keepdims=True)
-    grad_vecs[2:3, :] += jnp.sum(grad_normed, axis=0, keepdims=True)
-    grad_vecs[3:4, :] += jnp.sum(cot32, axis=0, keepdims=True)
+    sum_vecs[0:1, :] += jnp.sum(attended.astype(F32), axis=0, keepdims=True)
+    sum_vecs[1:2, :] += jnp.sum(grad_normed * xhat, axis=0, keepdims=True)
+    sum_vecs[2:3, :] += jnp.sum(grad_normed, axis=0, keepdims=True)
+    sum_vecs[3:4, :] += jnp.sum(cot32, axis=0, keepdims=True)
 
     @pl.when(step == pl.num_programs(0) - 1)
     def _():
-        grad_proj[...] = sum_proj[...].astype(BF16)
-        grad_expand[...] = sum_expand[...].astype(BF16)
-        grad_reduce[...] = sum_reduce[...].astype(BF16)
-
-
-def middle_all(tokens, mixed, cotangent, vecs, ebias, proj, expand, reduce, block=512, part=512):
+        proj[...] = sum_proj[...].astype(BF16)
+        expand[...] = sum_expand[...].astype(BF16)
+        reduce[...] = sum_reduce[...].astype(BF16)
+        blank[...] = jnp.zeros_like(blank)
+        per = hidden // width
+
+        def rows_of_shard(shard):
+            rows = [sum_vecs[0:4, shard * own : (shard + 1) * own]]
+            for index in range(per):
+                at = (shard * per + index) * own
+                rows.append(sum_ebias[0:1, at : at + own])
+            return jnp.concatenate(rows, axis=0)
+
+        small_blocks(rows_of_shard, small, 2 * chips, own)
+        run_copies(
+            spread_copies(
+                place,
+                [(proj, False), (expand, False), (reduce, True)],
+                small,
+                blank,
+                mine,
+                theirs,
+                chips,
+                out_sems,
+            )
+        )
+
+
+def middle_all(
+    place, tokens, mixed, cotangent, vecs, ebias, owns, pieces, split, block=512, part=512
+):
     rows, width = tokens.shape
-    row_block = pl.BlockSpec((block, width), lambda i: (i, 0))
+    chips = lax.axis_size("fsdp") // 2
+    hidden = ebias.shape[1]
+    height = width // (4 * chips)
+    row_block = pl.BlockSpec((block, width), lambda i, t: (i, 0))
     row_shape = jax.ShapeDtypeStruct((rows, width), BF16)
+    packed = (4 * chips * height, width // 2 + hidden // 2 + hidden // 2 + 128)
+    packed_shape = jax.ShapeDtypeStruct(packed, BF16)
+    sources = [*owns, *(core_swap(own) for own in owns), *pieces[0], *pieces[1]]
+    halves = hidden // width // 2
     return pl.pallas_call(
-        functools.partial(middle_kernel, part),
-        grid=(rows // block,),
-        in_specs=[
-            row_block,
-            row_block,
-            row_block,
-            resident(vecs.shape),
-            resident(ebias.shape),
-            resident(proj.shape),
-            resident(expand.shape),
-            resident(reduce.shape),
-        ],
-        out_specs=[
-            row_block,
-            row_block,
-            row_block,
-            resident(proj.shape),
-            resident(expand.shape),
-            resident(reduce.shape),
-            resident(ebias.shape),
-            resident((8, width)),
-        ],
-        out_shape=[
-            row_shape,
-            row_shape,
-            row_shape,
-            jax.ShapeDtypeStruct(proj.shape, BF16),
-            jax.ShapeDtypeStruct(expand.shape, BF16),
-            jax.ShapeDtypeStruct(reduce.shape, BF16),
-            jax.ShapeDtypeStruct(ebias.shape, F32),
-            jax.ShapeDtypeStruct((8, width), F32),
-        ],
-        scratch_shapes=[
-            pltpu.VMEM(proj.shape, F32),
-            pltpu.VMEM(expand.shape, F32),
-            pltpu.VMEM(reduce.shape, F32),
-        ],
+        functools.partial(middle_kernel, part, chips, split),
+        grid_spec=pltpu.PrefetchScalarGridSpec(
+            num_scalar_prefetch=1,
+            grid=(rows // block,),
+            in_specs=[row_block] * 3
+            + [
+                pl.BlockSpec(vecs.shape, lambda i, t: (0, 0)),
+                pl.BlockSpec(ebias.shape, lambda i, t: (0, 0)),
+            ]
+            + [hbm()] * len(sources),
+            out_specs=[row_block] * 3 + [hbm(), hbm()],
+            scratch_shapes=[
+                pltpu.VMEM((width, width), BF16),
+                pltpu.VMEM((width, hidden), BF16),
+                pltpu.VMEM((hidden, width), BF16),
+                pltpu.VMEM((width, width), F32),
+                pltpu.VMEM((width, hidden), F32),
+                pltpu.VMEM((hidden, width), F32),
+                pltpu.VMEM((1, hidden), F32),
+                pltpu.VMEM((8, width), F32),
+                pltpu.VMEM((2 * chips, height, 128), BF16),
+                pltpu.VMEM((height, 128), BF16),
+                pltpu.SemaphoreType.DMA((2 * (3 + 4 * (chips - 1) * (2 + halves)),)),
+                pltpu.SemaphoreType.DMA((8 * chips * (3 + halves),)),
+            ],
+        ),
+        out_shape=[row_shape, row_shape, row_shape, packed_shape, packed_shape],
         compiler_params=params(63),
-    )(tokens, mixed, cotangent, vecs, ebias, proj, expand, reduce)
-
-
-def weight_kernel(normed, dq, dk, dv, grad_weight, grad_vecs, total):
+        cost_estimate=pl.CostEstimate(
+            flops=6 * rows * width * (width + 2 * hidden),
+            bytes_accessed=40_000_000,
+            transcendentals=rows * hidden * 2,
+        ),
+    )(place, tokens, mixed, cotangent, vecs, ebias, *sources)
+
+
+def weight_kernel(
+    chips, place, unit, dq, dk, dv, vecs, weight, mine, theirs, total, sums, low, small, blank, sems
+):
     step = pl.program_id(0)
-    width = normed.shape[1]
+    width = unit.shape[1]
+    own = width // (2 * chips)
 
     @pl.when(step == 0)
     def _():
         total[...] = jnp.zeros_like(total)
-        grad_vecs[...] = jnp.zeros_like(grad_vecs)
-
-    rows_t = normed[...].T
+        sums[...] = jnp.zeros_like(sums)
+
+    rows_t = unit[...].T
     for index, part in enumerate((dq, dk, dv)):
-        total[:, index * width : (index + 1) * width] += dot(rows_t, part[...])
-    grad_vecs[0:1, :] += jnp.sum(dq[...].astype(F32), axis=0, keepdims=True)
-    grad_vecs[1:2, :] += jnp.sum(dv[...].astype(F32), axis=0, keepdims=True)
+        cols = slice(index * width, (index + 1) * width)
+        total[:, cols] += dot(rows_t, part[...])
+        sums[0:1, cols] += jnp.sum(part[...].astype(F32), axis=0, keepdims=True)
 
     @pl.when(step == pl.num_programs(0) - 1)
     def _():
-        grad_weight[...] = total[...].astype(BF16)
-
-
-def qkv_weight_grad(normed, dq, dk, dv, block=512):
-    rows, width = normed.shape
-    row_block = pl.BlockSpec((block, width), lambda i: (i, 0))
+        columns = vecs[...].T
+        gain, shift = columns[:, 0:1], columns[:, 1:2]
+        gain_part = jnp.zeros((width, 1), F32)
+        shift_part = jnp.zeros((width, 1), F32)
+        for index in range(3):
+            cols = slice(index * width, (index + 1) * width)
+            raw = total[:, cols]
+            sides = weight[:, cols].astype(F32)
+            line = sums[0:1, cols]
+            gain_part += jnp.sum(raw * sides, axis=1, keepdims=True)
+            shift_part += jnp.sum(line * sides, axis=1, keepdims=True)
+            low[:, cols] = (gain * raw + shift * line).astype(BF16)
+        pick = lax.broadcasted_iota(jnp.int32, (width, 128), 1)
+        both = jnp.where(pick == 0, gain_part, jnp.where(pick == 1, shift_part, 0.0)).T
+        blank[...] = jnp.zeros_like(blank)
+
+        def rows_of_shard(shard):
+            cols = slice(shard * own, (shard + 1) * own)
+            after = slice(2 * width + shard * own, 2 * width + (shard + 1) * own)
+            return jnp.concatenate([both[0:2, cols], sums[0:1, cols], sums[0:1, after]], axis=0)
+
+        small_blocks(rows_of_shard, small, 2 * chips, own)
+        run_copies(
+            spread_copies(place, [(low, False)], small, blank, mine, theirs, chips, sems)
+        )
+
+
+def qkv_weight_grad(place, unit, dq, dk, dv, vecs, weight, block=512):
+    rows, width = unit.shape
+    chips = lax.axis_size("fsdp") // 2
+    height = width // (4 * chips)
+    row_block = pl.BlockSpec((block, width), lambda i, t: (i, 0))
+    packed = jax.ShapeDtypeStruct((4 * chips * height, 3 * width // 2 + 128), BF16)
+    zero = lambda i, t: (0, 0)
     return pl.pallas_call(
-        weight_kernel,
-        grid=(rows // block,),
-        in_specs=[row_block] * 4,
-        out_specs=[resident((width, 3 * width)), resident((8, width))],
-        out_shape=[
-            jax.ShapeDtypeStruct((width, 3 * width), BF16),
-            jax.ShapeDtypeStruct((8, width), F32),
-        ],
-        scratch_shapes=[pltpu.VMEM((width, 3 * width), F32)],
-        compiler_params=params(40),
-    )(normed, dq, dk, dv)
-
-
-def input_kernel(tokens, grad_middle, dq, dk, dv, vecs, weight, input_grad, grad_vecs):
-    step = pl.program_id(0)
+        functools.partial(weight_kernel, chips),
+        grid_spec=pltpu.PrefetchScalarGridSpec(
+            num_scalar_prefetch=1,
+            grid=(rows // block,),
+            in_specs=[row_block] * 4
+            + [pl.BlockSpec(vecs.shape, zero), resident(weight.shape)],
+            out_specs=[hbm(), hbm()],
+            scratch_shapes=[
+                pltpu.VMEM((width, 3 * width), F32),
+                pltpu.VMEM((8, 3 * width), F32),
+                pltpu.VMEM((width, 3 * width), BF16),
+                pltpu.VMEM((2 * chips, height, 128), BF16),
+                pltpu.VMEM((height, 128), BF16),
+                pltpu.SemaphoreType.DMA((16 * chips,)),
+            ],
+        ),
+        out_shape=[packed, packed],
+        compiler_params=params(48),
+        cost_estimate=pl.CostEstimate(
+            flops=6 * rows * width * width, bytes_accessed=20_000_000, transcendentals=0
+        ),
+    )(place, unit, dq, dk, dv, vecs, weight)
+
+
+def input_kernel(tokens, grad_middle, dq, dk, dv, vecs, weight, input_grad):
     width = tokens.shape[1]
-
-    @pl.when(step == 0)
-    def _():
-        grad_vecs[...] = jnp.zeros_like(grad_vecs)
-
     xhat, scale = normalise(tokens[...].astype(F32))
     upstream = (
         dot_nt(dq[...], weight[:, :width])
@@ -598,8 +998,6 @@
     )
     grads = norm_back(upstream, vecs[0:1, :], xhat, scale)
     input_grad[...] = (grad_middle[...].astype(F32) + grads).astype(BF16)
-    grad_vecs[0:1, :] += jnp.sum(upstream * xhat, axis=0, keepdims=True)
-    grad_vecs[1:2, :] += jnp.sum(upstream, axis=0, keepdims=True)
 
 
 def input_backward(tokens, grad_middle, dq, dk, dv, vecs, weight, block=512):
@@ -609,12 +1007,12 @@
         input_kernel,
         grid=(rows // block,),
         in_specs=[row_block] * 5 + [resident(vecs.shape), resident(weight.shape)],
-        out_specs=[row_block, resident((8, width))],
-        out_shape=[
-            jax.ShapeDtypeStruct((rows, width), BF16),
-            jax.ShapeDtypeStruct((8, width), F32),
-        ],
+        out_specs=row_block,
+        out_shape=jax.ShapeDtypeStruct((rows, width), BF16),
         compiler_params=params(40),
+        cost_estimate=pl.CostEstimate(
+            flops=6 * rows * width * width, bytes_accessed=20_000_000, transcendentals=0
+        ),
     )(tokens, grad_middle, dq, dk, dv, vecs, weight)
 
 
@@ -638,8 +1036,18 @@
     reduce_bias,
 ):
     seq_len = segment_ids.shape[1]
-    own = norm1_gain.shape[0]
+    own, width = proj_weight.shape
+    shards = lax.axis_size("fsdp")
+    chips = shards // 2
+    height = own // 2
     per = expand_bias.shape[0] // own
+    place = place_table()
+    row_bit, col_bit = place[2], place[3]
+
+    def tile(weight):
+        half = weight.shape[1] // 2
+        return lax.dynamic_slice(weight, (row_bit * height, col_bit * half), (height, half))
+
     small = jnp.stack(
         [
             norm1_gain,
@@ -653,63 +1061,88 @@
             *jnp.split(expand_bias, per),
         ]
     )
-    small = lax.all_gather(small, "fsdp", axis=0)
-    shards = small.shape[0]
-    vecs = small[:, :8].swapaxes(0, 1).reshape(8, shards * own).astype(F32)
-    ebias = small[:, 8:].reshape(1, shards * own * per).astype(F32)
-    qkv_full = lax.all_gather(qkv_weight, "fsdp", axis=0, tiled=True)
-    proj_full = lax.all_gather(proj_weight, "fsdp", axis=0, tiled=True)
-    expand_full = lax.all_gather(expand_weight, "fsdp", axis=0, tiled=True)
-    reduce_full = lax.all_gather(reduce_weight, "fsdp", axis=0, tiled=True)
+    block = jnp.pad(small, ((0, height - small.shape[0]), (0, 128 - own)))
+    piece = jnp.concatenate([tile(qkv_weight), block], axis=1)
+    qkv_split = piece.shape[1] // 2
+    qkv_pieces = gather_pieces(piece, qkv_split)
+
+    quarter = lax.dynamic_slice(
+        reduce_weight,
+        ((row_bit * 2 + col_bit) * (per * own // 4), 0),
+        (per * own // 4, width),
+    )
+    parts = [tile(proj_weight), tile(expand_weight), *jnp.split(quarter, per // 2, axis=0)]
+    middle_split = (width + per * width) // 2
+    middle_pieces = gather_pieces(jnp.concatenate(parts, axis=1), middle_split)
+
+    chip, core = place[0], place[1]
+    edge = piece.shape[1] - 128
+
+    def blocks_of(first, along):
+        rest = along.reshape(chips - 1, height, -1)[:, : small.shape[0], edge : edge + own]
+        return jnp.concatenate([first[None], rest], axis=0)
+
+    both = jnp.stack(
+        [
+            blocks_of(small, qkv_pieces[0][0]),
+            blocks_of(core_swap(small), qkv_pieces[1][0]),
+        ],
+        axis=1,
+    )
+    hops = (chip - jnp.arange(chips)) % chips
+    choice = (hops[:, None, None, None] == jnp.arange(chips)[None, None, :, None]) & (
+        (jnp.arange(2) ^ core)[None, :, None, None] == jnp.arange(2)[None, None, None, :]
+    )
+    small = jnp.sum(
+        jnp.where(choice[..., None, None], both[None, None].astype(F32), 0.0), axis=(2, 3)
+    ).reshape(shards, small.shape[0], own)
+    vecs = small[:, :8].swapaxes(0, 1).reshape(8, width)
+    ebias = small[:, 8:].reshape(1, width * per)
 
     table = clip_table(segment_ids, valid_mask)
-    qkv, normed1 = qkv_forward(tokens, vecs, qkv_full)
+    qkv, unit, qkv_full = qkv_forward(place, tokens, vecs, qkv_weight, qkv_pieces, qkv_split)
     mixed, inverse, exps = attend_forward(table, qkv, seq_len)
-    (
-        output,
-        grad_middle,
-        grad_mixed,
-        grad_proj,
-        grad_expand,
-        grad_reduce,
-        grad_ebias,
-        middle_vecs,
-    ) = middle_all(tokens, mixed, cotangent, vecs, ebias, proj_full, expand_full, reduce_full)
-
-    def shard(grad):
-        part = lax.psum_scatter(grad, "fsdp", scatter_dimension=0, tiled=True)
-        return lax.psum(part, "rep").astype(F32)
-
-    sum_reduce = shard(grad_reduce)
-    sum_expand = shard(grad_expand)
-    sum_proj = shard(grad_proj)
+    output, grad_middle, grad_mixed, mine, theirs = middle_all(
+        place,
+        tokens,
+        mixed,
+        cotangent,
+        vecs,
+        ebias,
+        (proj_weight, expand_weight, reduce_weight),
+        middle_pieces,
+        middle_split,
+    )
+    sum_proj, sum_expand, sum_reduce, middle_small = sum_pieces(
+        place,
+        mine,
+        theirs,
+        mine.shape[1] // 256 * 128,
+        (False, False, True),
+        (proj_weight.shape, expand_weight.shape, reduce_weight.shape),
+    )
     dq, dk, dv = attend_backward(table, qkv, grad_mixed, mixed, inverse, exps, seq_len)
-    grad_qkv, qkv_vecs = qkv_weight_grad(normed1, dq, dk, dv)
-    sum_qkv = shard(grad_qkv)
-    input_grad, input_vecs = input_backward(tokens, grad_middle, dq, dk, dv, vecs, qkv_full)
-
-    vec_rows = jnp.concatenate([input_vecs[:2], qkv_vecs[:2], middle_vecs[:4]], axis=0)
-    vec_rows = vec_rows.reshape(8, shards, own).swapaxes(0, 1)
-    bias_rows = grad_ebias.reshape(shards, per, own)
-    small_grads = jnp.concatenate([vec_rows, bias_rows], axis=1)
-    small_grads = lax.psum(small_grads, "rep")
-    small_grads = lax.psum_scatter(small_grads, "fsdp", scatter_dimension=0)
+    mine, theirs = qkv_weight_grad(place, unit, dq, dk, dv, vecs, qkv_full)
+    sum_qkv, qkv_small = sum_pieces(
+        place, mine, theirs, mine.shape[1] // 256 * 128, (False,), (qkv_weight.shape,)
+    )
+    input_grad = input_backward(tokens, grad_middle, dq, dk, dv, vecs, qkv_full)
     return (
         output,
         input_grad,
-        small_grads[0],
-        small_grads[1],
+        qkv_small[0, :own],
+        qkv_small[1, :own],
         sum_qkv,
-        small_grads[2],
-        small_grads[3],
+        qkv_small[2, :own],
+        qkv_small[3, :own],
         sum_proj,
-        small_grads[4],
-        small_grads[5],
-        small_grads[6],
+        middle_small[0, :own],
+        middle_small[1, :own],
+        middle_small[2, :own],
         sum_expand,
-        small_grads[8:].reshape(-1),
+        middle_small[4 : 4 + per, :own].reshape(-1),
         sum_reduce,
-        small_grads[7],
+        middle_small[3, :own],
     )
 
 

time: 634 us -> 492 us (0.78)
  waiting for transfers between devices: 324 us -> 140 us
  starting transfers between devices: 0.39 us -> 53.3 us
  Pallas kernels: 227 us -> 260 us
  blocking collectives: 26 us -> 0 us
  between operations: 14.5 us -> 1.36 us
  other arithmetic: 9.34 us -> 2.54 us
    reduce_scatter x5 -> x0, waiting for transfers between devices: 161 us -> none  [the longest x4 130 us: shard(): part = lax.psum_scatter(grad, 'fsdp', scatter_dimension=0, tiled=True)]
    ppermute x0 -> x51, waiting for transfers between devices: none -> 140 us  [the longest x22 88.1 us: replica_swap(): return lax.ppermute(value, 'rep', [(i, i ^ bits) for i in range(4)])]
    all_gather x4 -> x0, waiting for transfers between devices: 104 us -> none  [the longest x1 52 us: local(): reduce_full = lax.all_gather(reduce_weight, 'fsdp', axis=0, tiled=True)]
    psum x1 -> x0, waiting for transfers between devices: 54.8 us -> none  [shard(): return lax.psum(part, 'rep').astype(F32)]
    ppermute x0 -> x51, starting transfers between devices: none -> 53.3 us  [the longest x12 27.2 us: chip_shift(): lax.ppermute(value, 'fsdp', [(i, (i + 2 * hops) % count) for i in range(c...]
    pallas_call x3 -> x13, Pallas kernels: 126 us -> 159 us  [the longest x1 113 us: middle_all(): pl.pallas_call(functools.partial(middle_kernel, part, chips, split), grid...]
    all_gather x1 -> x0, blocking collectives: 15.8 us -> none  [local(): small = lax.all_gather(small, 'fsdp', axis=0)]
    psum x1 -> x0, blocking collectives: 10.2 us -> none  [local(): small_grads = lax.psum(small_grads, 'rep')]
  transfers between devices with their start and end apart: 10 -> 51, of which waited for: 8 -> 15; matrix products, arithmetic and copies ran while one was open for 1% -> 3% of each run, Pallas kernels for 20% -> 30%
where the time goes in v2:
time: 492 us; the launch traced here: 484 us
  Pallas kernels  260 us (53%)
  waiting for transfers between devices  140 us (28%)
  starting transfers between devices  53.3 us (11%)
  local copies, waits for them, and re-layouts  27.9 us (6%)
    pallas_call x1, Pallas kernels, middle_all(): pl.pallas_call(functools.partial(middle_kernel, part, chips, split), grid...  113 us
    ppermute x22, waiting for transfers between devices, replica_swap(): return lax.ppermute(value, 'rep', [(i, i ^ bits) for i in range(4)])  88.1 us
    pallas_call x1, Pallas kernels, attend_backward(): pl.pallas_call(functools.partial(back_kernel, pairs), grid_spec=pltpu.Pre...  57.2 us
    ppermute x12, waiting for transfers between devices, chip_shift(): lax.ppermute(value, 'fsdp', [(i, (i + 2 * hops) % count) for i in range(c...  50.1 us
    pallas_call x1, Pallas kernels, attend_forward(): pl.pallas_call(functools.partial(attend_kernel, pairs), grid_spec=pltpu.P...  29.5 us
    ppermute x12, starting transfers between devices, chip_shift(): lax.ppermute(value, 'fsdp', [(i, (i + 2 * hops) % count) for i in range(c...  27.2 us
    ppermute x22, starting transfers between devices, replica_swap(): return lax.ppermute(value, 'rep', [(i, i ^ bits) for i in range(4)])  23.3 us
    pallas_call x1, Pallas kernels, qkv_weight_grad(): pl.pallas_call(functools.partial(weight_kernel, chips), grid_spec=pltpu.P...  17.8 us
  transfers between devices with their start and end apart: 51, of which 15 were waited for; matrix products, arithmetic and copies ran while one was open for 3% of the time, Pallas kernels for 30%

profile of v2, /device:TPU:0, one launch (start us, length us, event | category | flops | bytes accessed | tf_op | source)
XLA Modules:
  0.0 484.4 jit_solution(15602965247348588572)
XLA Ops:
  3.3 3.1 collective-permute-start
  6.4 2.6 collective-permute-start.1
  9.0 1.3 collective-permute-start.2
  15.8 1.2 collective-permute-start.17
  17.1 1.9 collective-permute-start.18
  19.0 3.5 collective-permute-start.19
  22.5 5.9 %collective-permute-done.17 = bf16[48,3456]{1,0:T(8,128)(2,1)S(1)} collective-permute-done((bf16[48,3456]{1,0:T(8,128)(2,1)S(1)}, bf16[48,3456]{1,0:T(8,128)(2,1)S(1)}, u32[]{:S(2)}, u32[]{:S(2)}) %collective-permute-start.17) | collective-permute-done | bytes 331808 | tf_op jit(solution)/shard_map/ppermute | solution.py:67
  29.2 12.5 %collective-permute-done.18 = bf16[48,3456]{1,0:T(8,128)(2,1)S(1)} collective-permute-done((bf16[48,3456]{1,0:T(8,128)(2,1)S(1)}, bf16[48,3456]{1,0:T(8,128)(2,1)S(1)}, u32[]{:S(2)}, u32[]{:S(2)}) %collective-permute-start.18) | collective-permute-done | bytes 331808 | tf_op jit(solution)/shard_map/ppermute | solution.py:67
  41.7 1.5 collective-permute-start.6
  43.9 1.5 collective-permute-start.7
  47.4 5.7 %collective-permute-done.6.refs_3_ = bf16[144,1280]{1,0:T(8,128)(2,1)S(1)} collective-permute-done((bf16[144,1280]{1,0:T(8,128)(2,1)S(1)}, bf16[144,1280]{1,0:T(8,128)(2,1)S(1)}, u32[]{:S(2)}, u32[]{:S(2)}) %collective-permute-start.6) | collective-permute-done | bytes 368672 | tf_op jit(solution)/shard_map/ppermute | solution.py:71
  53.1 2.3 collective-permute-done.7.refs_4_
  55.6 1.5 collective-permute-done.4.refs_7_
  57.1 1.5 collective-permute-start.8
  59.9 19.4 %collective-permute-done.8.refs_5_ = bf16[144,640]{1,0:T(8,128)(2,1)S(1)} collective-permute-done((bf16[144,640]{1,0:T(8,128)(2,1)S(1)}, bf16[144,640]{1,0:T(8,128)(2,1)S(1)}, u32[]{:S(2)}, u32[]{:S(2)}) %collective-permute-start.8) | collective-permute-done | bytes 184352 | tf_op jit(solution)/shard_map/ppermute | solution.py:71
  80.0 1.9 slice.74
  82.0 1.6 collective-permute-start.22
  83.6 1.8 slice.75
  89.2 8.8 %collective-permute-done.23.refs_10_ = bf16[144,1536]{1,0:T(8,128)(2,1)} collective-permute-done((bf16[144,1536]{1,0:T(8,128)(2,1)}, bf16[144,1536]{1,0:T(8,128)(2,1)}, u32[]{:S(2)}, u32[]{:S(2)}) %collective-permute-start.23) | collective-permute-done | bytes 442400 | tf_op jit(solution)/shard_map/ppermute | solution.py:71
  98.5 1.9 copy-done.6
  101.3 14.1 %shard_map.280 = (bf16[2048,2304]{1,0:T(8,128)(2,1)}, bf16[2048,768]{1,0:T(8,128)(2,1)S(1)}, bf16[768,2304]{1,0:T(8,128)(2,1)S(1)}) custom-call(s32[4]{0:T(128)S(1)} %pad_add_fusion.place.table, bf16[2048,768]{1,0:T(8,128)(2,1)S(1)} %copy-done.6, f32[8,768]{1,0:T(8,128)S(1)} %reshape.284.vecs, bf16[96,2304]{1,0:T(8,128)(2,1)S(1)} %copy-done.3, ...), custom_call_target="tpu_custom_call" | custom-call | flops 7247757312 | bytes 20000000 | tf_op jit(solution)/shard_map/pallas_call | solution.py:379
  115.4 1.8 copy-done.13
  117.2 1.7 copy-done.15
  118.9 29.5 %shard_map.281 = (bf16[2048,768]{1,0:T(8,128)(2,1)S(1)}, f32[2048,768]{1,0:T(8,128)}, bf16[2,12,1536,256]{3,2,1,0:T(8,128)(2,1)}) custom-call(s32[60]{0:T(128)S(1)} %reshape.280.table, bf16[2048,2304]{1,0:T(8,128)(2,1)} %get-tuple-element.61.queries.keys.values, bf16[2048,2304]{1,0:T(8,128)(2,1)} %get-tuple-element.61.queries.keys.values, ...), custom_call_target="tpu_custom_call" | custom-call | tf_op jit(solution)/shard_map/pallas_call | solution.py:545
  148.4 1.7 copy-done
  150.1 113.3 %shard_map.282 = (bf16[2048,768]{1,0:T(8,128)(2,1)}, bf16[2048,768]{1,0:T(8,128)(2,1)}, bf16[2048,768]{1,0:T(8,128)(2,1)}, bf16[768,3584]{1,0:T(8,128)(2,1)}, bf16[768,3584]{1,0:T(8,128)(2,1)}) custom-call(s32[4]{0:T(128)} %copy-done.1, bf16[2048,768]{1,0:T(8,128)(2,1)} %tokens.5, bf16[2048,768]{1,0:T(8,128)(2,1)} %copy-done, bf16[2048,768]{1,0:T(8,128)(2,1)} %cotangent.1, ...), custom_call_target="tpu_custom_call" | custom-call | flops 65229815808 | bytes 40000000 | tf_op jit(solution)/shard_map/pallas_call | solution.py:875
  263.5 57.2 %shard_map.283 = (bf16[2048,768]{1,0:T(8,128)(2,1)S(1)}, bf16[2048,768]{1,0:T(8,128)(2,1)}, bf16[2048,768]{1,0:T(8,128)(2,1)}) custom-call(s32[60]{0:T(128)S(1)} %reshape.280.table, bf16[2048,2304]{1,0:T(8,128)(2,1)} %get-tuple-element.61.queries.keys.values, bf16[2048,2304]{1,0:T(8,128)(2,1)} %get-tuple-element.61.queries.keys.values, ...), custom_call_target="tpu_custom_call" | custom-call | tf_op jit(solution)/shard_map/pallas_call | solution.py:704
  320.6 1.7 copy-done.8
  322.3 17.8 %shard_map.285 = (bf16[768,1280]{1,0:T(8,128)(2,1)S(1)}, bf16[768,1280]{1,0:T(8,128)(2,1)S(1)}) custom-call(s32[4]{0:T(128)S(1)} %copy-done.2, bf16[2048,768]{1,0:T(8,128)(2,1)} %copy-done.15, bf16[2048,768]{1,0:T(8,128)(2,1)} %copy-done.8, bf16[2048,768]{1,0:T(8,128)(2,1)} %get-tuple-element.69.dk, bf16[2048,768]{1,0:T(8,128)(2,1)} %get-tuple-element.70.dv, ...), custom_call_target="tpu_custom_call" | custom-call | flops 7247757312 | bytes 20000000 | tf_op jit(solution)/shard_map/pallas_call | solution.py:966
  340.6 4.5 shard_map.291
  347.2 1.6 collective-permute-start.30
  348.7 1.7 collective-permute-start.31
  350.4 27.8 %collective-permute-done.41.got_a = bf16[384,1792]{1,0:T(8,128)(2,1)S(1)} collective-permute-done((bf16[384,1792]{1,0:T(8,128)(2,1)S(1)}, bf16[384,1792]{1,0:T(8,128)(2,1)S(1)}, u32[]{:S(2)}, u32[]{:S(2)}) %collective-permute-start.41) | collective-permute-done | bytes 1376288 | tf_op jit(solution)/shard_map/ppermute | solution.py:71
  378.7 1.3 shard_map.292
  380.4 1.5 collective-permute-start.44
  381.9 6.8 %collective-permute-done.30.got_a = bf16[384,640]{1,0:T(8,128)(2,1)S(1)} collective-permute-done((bf16[384,640]{1,0:T(8,128)(2,1)S(1)}, bf16[384,640]{1,0:T(8,128)(2,1)S(1)}, u32[]{:S(2)}, u32[]{:S(2)}) %collective-permute-start.30) | collective-permute-done | bytes 491552 | tf_op jit(solution)/shard_map/ppermute | solution.py:71
  390.6 1.5 collective-permute-start.33
  392.0 16.1 %collective-permute-done.32.got_a = bf16[192,640]{1,0:T(8,128)(2,1)S(1)} collective-permute-done((bf16[192,640]{1,0:T(8,128)(2,1)S(1)}, bf16[192,640]{1,0:T(8,128)(2,1)S(1)}, u32[]{:S(2)}, u32[]{:S(2)}) %collective-permute-start.32) | collective-permute-done | bytes 245792 | tf_op jit(solution)/shard_map/ppermute | solution.py:71
  408.8 6.8 %collective-permute-start.34 = (bf16[48,1280]{1,0:T(8,128)(2,1)S(1)}, bf16[48,1280]{1,0:T(8,128)(2,1)S(1)}, u32[]{:S(2)}, u32[]{:S(2)}) collective-permute-start(bf16[48,1280]{1,0:T(8,128)(2,1)S(1)} %get-tuple-element.84), channel_id=1, source_target_pairs={{0,2},{1,3},{2,4},{3,5},{4,6},{5,7},{6,0},{7,1},{8,10},{9,11},{10,... | collective-permute-start | bytes 368648 | tf_op jit(solution)/shard_map/ppermute | solution.py:67
  416.6 3.7 collective-permute-start.47
  420.3 2.0 collective-permute-start.35
  423.2 31.5 %collective-permute-done.35.refs_2_ = bf16[48,1280]{1,0:T(8,128)(2,1)S(1)} collective-permute-done((bf16[48,1280]{1,0:T(8,128)(2,1)S(1)}, bf16[48,1280]{1,0:T(8,128)(2,1)S(1)}, u32[]{:S(2)}, u32[]{:S(2)}) %collective-permute-start.35) | collective-permute-done | bytes 122912 | tf_op jit(solution)/shard_map/ppermute | solution.py:67
  456.7 2.3 collective-permute-start.39
  461.1 2.1 collective-permute-start.50
  463.2 1.9 copy-done.14
  465.1 13.6 %shard_map.284 = bf16[2048,768]{1,0:T(8,128)(2,1)} custom-call(bf16[2048,768]{1,0:T(8,128)(2,1)S(1)} %copy-done.7, bf16[2048,768]{1,0:T(8,128)(2,1)S(1)} %copy-done.14, bf16[2048,768]{1,0:T(8,128)(2,1)S(1)} %copy-done.9, bf16[2048,768]{1,0:T(8,128)(2,1)S(1)} %copy-done.10, bf16[2048,768]{1,0:T(8,128)(2,1)} %get-tuple-element.70.dv, f32[8,768]{1,0:T(8,128)S(1)} %copy-done.5, ...), custom_call_target="tpu_custom_call" | custom-call | flops 7247757312 | bytes 20000000 | tf_op jit(solution)/shard_map/pallas_call | solution.py:1006
  478.7 1.5 shard_map.290
  480.8 2.2 shard_map.295
  (165 shorter events, 32.8 us)
Async XLA Ops:
  3.3 12.4 %collective-permute-start = (bf16[48,1280]{1,0:T(8,128)(2,1)S(1)}, bf16[48,1280]{1,0:T(8,128)(2,1)S(1)}, u32[]{:S(2)}, u32[]{:S(2)}) collective-permute-start(bf16[48,1280]{1,0:T(8,128)(2,1)S(1)} %fusion.1), channel_id=1, source_target_pairs={{0,2},{1,3},{2,4},{3,5},{4,6},{5,7},{6,0},{7,1},{8,10},{9,11},{10,... | collective-permute-start | bytes 368648 | tf_op jit(solution)/shard_map/ppermute | solution.py:67
  6.4 10.7 %collective-permute-start.1 = (bf16[48,1280]{1,0:T(8,128)(2,1)S(1)}, bf16[48,1280]{1,0:T(8,128)(2,1)S(1)}, u32[]{:S(2)}, u32[]{:S(2)}) collective-permute-start(bf16[48,1280]{1,0:T(8,128)(2,1)S(1)} %fusion.1), channel_id=1, source_target_pairs={{0,4},{1,5},{2,6},{3,7},{4,0},{5,1},{6,2},{7,3},{8,12},{9,13},{10,... | collective-permute-start | bytes 368648 | tf_op jit(solution)/shard_map/ppermute | solution.py:67
  9.0 10.0 %collective-permute-start.2 = (bf16[48,1280]{1,0:T(8,128)(2,1)S(1)}, bf16[48,1280]{1,0:T(8,128)(2,1)S(1)}, u32[]{:S(2)}, u32[]{:S(2)}) collective-permute-start(bf16[48,1280]{1,0:T(8,128)(2,1)S(1)} %fusion.1), channel_id=1, source_target_pairs={{0,6},{1,7},{2,0},{3,1},{4,2},{5,3},{6,4},{7,5},{8,14},{9,15},{10,... | collective-permute-start | bytes 368648 | tf_op jit(solution)/shard_map/ppermute | solution.py:67
  10.3 35.8 %collective-permute-start.3 = (bf16[12,96]{1,0:T(8,128)(2,1)S(1)}, bf16[12,96]{1,0:T(8,128)(2,1)S(1)}, u32[]{:S(2)}, u32[]{:S(2)}) collective-permute-start(bf16[12,96]{1,0:T(8,128)(2,1)S(1)} %stack.89), channel_id=1, source_target_pairs={{0,1},{1,0},{2,3},{3,2},{4,5},{5,4},{6,7},{7,6},{8,9},{9,8},{10,11... | collective-permute-start | bytes 6920 | tf_op jit(solution)/shard_map/ppermute | solution.py:62
  10.4 37.0 %collective-permute-start.5 = (bf16[96,2304]{1,0:T(8,128)(2,1)}, bf16[96,2304]{1,0:T(8,128)(2,1)S(1)}, u32[]{:S(2)}, u32[]{:S(2)}) collective-permute-start(bf16[96,2304]{1,0:T(8,128)(2,1)} %refs_0_.2), channel_id=1, source_target_pairs={{0,1},{1,0},{2,3},{3,2},{4,5},{5,4},{6,7},{7,6},{8,9},{9,8},{10,11... | collective-permute-start | bytes 1327112 | tf_op jit(solution)/shard_map/ppermute | solution.py:62
  15.8 12.6 %collective-permute-start.17 = (bf16[48,3456]{1,0:T(8,128)(2,1)S(1)}, bf16[48,3456]{1,0:T(8,128)(2,1)S(1)}, u32[]{:S(2)}, u32[]{:S(2)}) collective-permute-start(bf16[48,3456]{1,0:T(8,128)(2,1)S(1)} %pad_maximum_fusion), channel_id=1, source_target_pairs={{0,2},{1,3},{2,4},{3,5},{4,6},{5,7},{6,0},{7,1},{8,10},{9,11},{10,... | collective-permute-start | bytes 995336 | tf_op jit(solution)/shard_map/ppermute | solution.py:67
  17.1 24.5 %collective-permute-start.18 = (bf16[48,3456]{1,0:T(8,128)(2,1)S(1)}, bf16[48,3456]{1,0:T(8,128)(2,1)S(1)}, u32[]{:S(2)}, u32[]{:S(2)}) collective-permute-start(bf16[48,3456]{1,0:T(8,128)(2,1)S(1)} %pad_maximum_fusion), channel_id=1, source_target_pairs={{0,4},{1,5},{2,6},{3,7},{4,0},{5,1},{6,2},{7,3},{8,12},{9,13},{10,... | collective-permute-start | bytes 995336 | tf_op jit(solution)/shard_map/ppermute | solution.py:67
  19.0 24.9 %collective-permute-start.19 = (bf16[48,3456]{1,0:T(8,128)(2,1)S(1)}, bf16[48,3456]{1,0:T(8,128)(2,1)S(1)}, u32[]{:S(2)}, u32[]{:S(2)}) collective-permute-start(bf16[48,3456]{1,0:T(8,128)(2,1)S(1)} %pad_maximum_fusion), channel_id=1, source_target_pairs={{0,6},{1,7},{2,0},{3,1},{4,2},{5,3},{6,4},{7,5},{8,14},{9,15},{10,... | collective-permute-start | bytes 995336 | tf_op jit(solution)/shard_map/ppermute | solution.py:67
  28.4 18.4 %collective-permute-start.14 = (bf16[96,768]{1,0:T(8,128)(2,1)}, bf16[96,768]{1,0:T(8,128)(2,1)S(1)}, u32[]{:S(2)}, u32[]{:S(2)}) collective-permute-start(bf16[96,768]{1,0:T(8,128)(2,1)} %refs_0_.3), channel_id=1, source_target_pairs={{0,1},{1,0},{2,3},{3,2},{4,5},{5,4},{6,7},{7,6},{8,9},{9,8},{10,11... | collective-permute-start | bytes 442376 | tf_op jit(solution)/shard_map/ppermute | solution.py:62
  41.7 11.5 %collective-permute-start.6 = (bf16[144,1280]{1,0:T(8,128)(2,1)S(1)}, bf16[144,1280]{1,0:T(8,128)(2,1)S(1)}, u32[]{:S(2)}, u32[]{:S(2)}) collective-permute-start(bf16[144,1280]{1,0:T(8,128)(2,1)S(1)} %constant_dynamic-update-slice_fusion.5.refs_2_), channel_id=1, source_target_pairs={{0,8},{8,0},{16,24},{24,16},{1,9},{9,1},{17,25},{25,17},{2,10},{10... | collective-permute-start | bytes 1105928 | tf_op jit(solution)/shard_map/ppermute | solution.py:71
  43.9 11.5 %collective-permute-start.7 = (bf16[144,1280]{1,0:T(8,128)(2,1)S(1)}, bf16[144,1280]{1,0:T(8,128)(2,1)S(1)}, u32[]{:S(2)}, u32[]{:S(2)}) collective-permute-start(bf16[144,1280]{1,0:T(8,128)(2,1)S(1)} %constant_dynamic-update-slice_fusion.5.refs_2_), channel_id=1, source_target_pairs={{0,16},{8,24},{16,0},{24,8},{1,17},{9,25},{17,1},{25,9},{2,18},{10... | collective-permute-start | bytes 1105928 | tf_op jit(solution)/shard_map/ppermute | solution.py:71
  46.2 33.2 %collective-permute-start.20 = (bf16[144,3456]{1,0:T(8,128)(2,1)}, bf16[144,3456]{1,0:T(8,128)(2,1)}, u32[]{:S(2)}, u32[]{:S(2)}) collective-permute-start(bf16[144,3456]{1,0:T(8,128)(2,1)} %constant_dynamic-update-slice_fusion.8.refs_6_), channel_id=1, source_target_pairs={{0,8},{8,0},{16,24},{24,16},{1,9},{9,1},{17,25},{25,17},{2,10},{10... | collective-permute-start | bytes 2985992 | tf_op jit(solution)/shard_map/ppermute | solution.py:71
  46.8 35.2 %collective-permute-start.21 = (bf16[144,3456]{1,0:T(8,128)(2,1)}, bf16[144,3456]{1,0:T(8,128)(2,1)}, u32[]{:S(2)}, u32[]{:S(2)}) collective-permute-start(bf16[144,3456]{1,0:T(8,128)(2,1)} %constant_dynamic-update-slice_fusion.8.refs_6_), channel_id=1, source_target_pairs={{0,16},{8,24},{16,0},{24,8},{1,17},{9,25},{17,1},{25,9},{2,18},{10... | collective-permute-start | bytes 2985992 | tf_op jit(solution)/shard_map/ppermute | solution.py:71
  47.3 12.0 %collective-permute-start.15 = (bf16[96,3072]{1,0:T(8,128)(2,1)}, bf16[96,3072]{1,0:T(8,128)(2,1)S(1)}, u32[]{:S(2)}, u32[]{:S(2)}) collective-permute-start(bf16[96,3072]{1,0:T(8,128)(2,1)} %refs_1_.1), channel_id=1, source_target_pairs={{0,1},{1,0},{2,3},{3,2},{4,5},{5,4},{6,7},{7,6},{8,9},{9,8},{10,11... | collective-permute-start | bytes 1769480 | tf_op jit(solution)/shard_map/ppermute | solution.py:62
  53.1 6.8 %collective-permute-start.16 = (bf16[384,768]{1,0:T(8,128)(2,1)}, bf16[384,768]{1,0:T(8,128)(2,1)S(1)}, u32[]{:S(2)}, u32[]{:S(2)}) collective-permute-start(bf16[384,768]{1,0:T(8,128)(2,1)} %refs_2_.1), channel_id=1, source_target_pairs={{0,1},{1,0},{2,3},{3,2},{4,5},{5,4},{6,7},{7,6},{8,9},{9,8},{10,11... | collective-permute-start | bytes 1769480 | tf_op jit(solution)/shard_map/ppermute | solution.py:62
  57.1 22.2 %collective-permute-start.8 = (bf16[144,640]{1,0:T(8,128)(2,1)S(1)}, bf16[144,640]{1,0:T(8,128)(2,1)S(1)}, u32[]{:S(2)}, u32[]{:S(2)}) collective-permute-start(bf16[144,640]{1,0:T(8,128)(2,1)S(1)} %slice.71), channel_id=1, source_target_pairs={{0,16},{8,24},{16,0},{24,8},{1,17},{9,25},{17,1},{25,9},{2,18},{10... | collective-permute-start | bytes 552968 | tf_op jit(solution)/shard_map/ppermute | solution.py:71
  59.3 22.6 %collective-permute-start.9 = (bf16[144,640]{1,0:T(8,128)(2,1)}, bf16[144,640]{1,0:T(8,128)(2,1)S(1)}, u32[]{:S(2)}, u32[]{:S(2)}) collective-permute-start(bf16[144,640]{1,0:T(8,128)(2,1)} %slice.72), channel_id=1, source_target_pairs={{0,8},{8,0},{16,24},{24,16},{1,9},{9,1},{17,25},{25,17},{2,10},{10... | collective-permute-start | bytes 552968 | tf_op jit(solution)/shard_map/ppermute | solution.py:71
  59.9 26.2 %collective-permute-start.10 = (bf16[144,1280]{1,0:T(8,128)(2,1)S(1)}, bf16[144,1280]{1,0:T(8,128)(2,1)S(1)}, u32[]{:S(2)}, u32[]{:S(2)}) collective-permute-start(bf16[144,1280]{1,0:T(8,128)(2,1)S(1)} %collective-permute-done.6.refs_3_), channel_id=1, source_target_pairs={{0,1},{1,0},{2,3},{3,2},{4,5},{5,4},{6,7},{7,6},{8,9},{9,8},{10,11... | collective-permute-start | bytes 1105928 | tf_op jit(solution)/shard_map/ppermute | solution.py:62
  79.3 7.3 %collective-permute-start.11 = (bf16[144,1280]{1,0:T(8,128)(2,1)S(1)}, bf16[144,1280]{1,0:T(8,128)(2,1)S(1)}, u32[]{:S(2)}, u32[]{:S(2)}) collective-permute-start(bf16[144,1280]{1,0:T(8,128)(2,1)S(1)} %collective-permute-done.7.refs_4_), channel_id=1, source_target_pairs={{0,1},{1,0},{2,3},{3,2},{4,5},{5,4},{6,7},{7,6},{8,9},{9,8},{10,11... | collective-permute-start | bytes 1105928 | tf_op jit(solution)/shard_map/ppermute | solution.py:62
  79.3 6.1 %collective-permute-start.12 = (bf16[144,640]{1,0:T(8,128)(2,1)S(1)}, bf16[144,640]{1,0:T(8,128)(2,1)}, u32[]{:S(2)}, u32[]{:S(2)}) collective-permute-start(bf16[144,640]{1,0:T(8,128)(2,1)S(1)} %collective-permute-done.8.refs_5_), channel_id=1, source_target_pairs={{0,1},{1,0},{2,3},{3,2},{4,5},{5,4},{6,7},{7,6},{8,9},{9,8},{10,11... | collective-permute-start | bytes 552968 | tf_op jit(solution)/shard_map/ppermute | solution.py:62
  82.0 16.0 %collective-permute-start.22 = (bf16[144,1920]{1,0:T(8,128)(2,1)}, bf16[144,1920]{1,0:T(8,128)(2,1)}, u32[]{:S(2)}, u32[]{:S(2)}) collective-permute-start(bf16[144,1920]{1,0:T(8,128)(2,1)} %slice.74), channel_id=1, source_target_pairs={{0,16},{8,24},{16,0},{24,8},{1,17},{9,25},{17,1},{25,9},{2,18},{10... | collective-permute-start | bytes 1658888 | tf_op jit(solution)/shard_map/ppermute | solution.py:71
  85.4 12.6 %collective-permute-start.23 = (bf16[144,1536]{1,0:T(8,128)(2,1)}, bf16[144,1536]{1,0:T(8,128)(2,1)}, u32[]{:S(2)}, u32[]{:S(2)}) collective-permute-start(bf16[144,1536]{1,0:T(8,128)(2,1)} %slice.75), channel_id=1, source_target_pairs={{0,8},{8,0},{16,24},{24,16},{1,9},{9,1},{17,25},{25,17},{2,10},{10... | collective-permute-start | bytes 1327112 | tf_op jit(solution)/shard_map/ppermute | solution.py:71
  86.0 64.0 %collective-permute-start.24 = (bf16[144,3456]{1,0:T(8,128)(2,1)}, bf16[144,3456]{1,0:T(8,128)(2,1)}, u32[]{:S(2)}, u32[]{:S(2)}) collective-permute-start(bf16[144,3456]{1,0:T(8,128)(2,1)} %constant_dynamic-update-slice_fusion.8.refs_6_), channel_id=1, source_target_pairs={{0,1},{1,0},{2,3},{3,2},{4,5},{5,4},{6,7},{7,6},{8,9},{9,8},{10,11... | collective-permute-start | bytes 2985992 | tf_op jit(solution)/shard_map/ppermute | solution.py:62
  86.1 63.9 %collective-permute-start.25 = (bf16[144,3456]{1,0:T(8,128)(2,1)}, bf16[144,3456]{1,0:T(8,128)(2,1)}, u32[]{:S(2)}, u32[]{:S(2)}) collective-permute-start(bf16[144,3456]{1,0:T(8,128)(2,1)} %collective-permute-done.20.refs_7_), channel_id=1, source_target_pairs={{0,1},{1,0},{2,3},{3,2},{4,5},{5,4},{6,7},{7,6},{8,9},{9,8},{10,11... | collective-permute-start | bytes 2985992 | tf_op jit(solution)/shard_map/ppermute | solution.py:62
  86.6 63.4 %collective-permute-start.26 = (bf16[144,3456]{1,0:T(8,128)(2,1)}, bf16[144,3456]{1,0:T(8,128)(2,1)}, u32[]{:S(2)}, u32[]{:S(2)}) collective-permute-start(bf16[144,3456]{1,0:T(8,128)(2,1)} %collective-permute-done.21.refs_8_), channel_id=1, source_target_pairs={{0,1},{1,0},{2,3},{3,2},{4,5},{5,4},{6,7},{7,6},{8,9},{9,8},{10,11... | collective-permute-start | bytes 2985992 | tf_op jit(solution)/shard_map/ppermute | solution.py:62
  98.0 52.0 %collective-permute-start.28 = (bf16[144,1536]{1,0:T(8,128)(2,1)}, bf16[144,1536]{1,0:T(8,128)(2,1)}, u32[]{:S(2)}, u32[]{:S(2)}) collective-permute-start(bf16[144,1536]{1,0:T(8,128)(2,1)} %collective-permute-done.23.refs_10_), channel_id=1, source_target_pairs={{0,1},{1,0},{2,3},{3,2},{4,5},{5,4},{6,7},{7,6},{8,9},{9,8},{10,11... | collective-permute-start | bytes 1327112 | tf_op jit(solution)/shard_map/ppermute | solution.py:62
  98.0 52.1 %collective-permute-start.27 = (bf16[144,1920]{1,0:T(8,128)(2,1)}, bf16[144,1920]{1,0:T(8,128)(2,1)}, u32[]{:S(2)}, u32[]{:S(2)}) collective-permute-start(bf16[144,1920]{1,0:T(8,128)(2,1)} %collective-permute-done.22.refs_9_), channel_id=1, source_target_pairs={{0,1},{1,0},{2,3},{3,2},{4,5},{5,4},{6,7},{7,6},{8,9},{9,8},{10,11... | collective-permute-start | bytes 1658888 | tf_op jit(solution)/shard_map/ppermute | solution.py:62
  263.4 77.2 %collective-permute-start.40 = (bf16[768,3584]{1,0:T(8,128)(2,1)}, bf16[768,3584]{1,0:T(8,128)(2,1)}, u32[]{:S(2)}, u32[]{:S(2)}) collective-permute-start(bf16[768,3584]{1,0:T(8,128)(2,1)} %get-tuple-element.90), channel_id=1, source_target_pairs={{0,1},{1,0},{2,3},{3,2},{4,5},{5,4},{6,7},{7,6},{8,9},{9,8},{10,11... | collective-permute-start | bytes 16515080 | tf_op jit(solution)/shard_map/ppermute | solution.py:62
  340.1 6.0 %collective-permute-start.29 = (bf16[768,1280]{1,0:T(8,128)(2,1)S(1)}, bf16[768,1280]{1,0:T(8,128)(2,1)S(1)}, u32[]{:S(2)}, u32[]{:S(2)}) collective-permute-start(bf16[768,1280]{1,0:T(8,128)(2,1)S(1)} %get-tuple-element.74), channel_id=1, source_target_pairs={{0,1},{1,0},{2,3},{3,2},{4,5},{5,4},{6,7},{7,6},{8,9},{9,8},{10,11... | collective-permute-start | bytes 5898248 | tf_op jit(solution)/shard_map/ppermute | solution.py:62
  345.1 33.1 %collective-permute-start.41 = (bf16[384,1792]{1,0:T(8,128)(2,1)S(1)}, bf16[384,1792]{1,0:T(8,128)(2,1)S(1)}, u32[]{:S(2)}, u32[]{:S(2)}) collective-permute-start(bf16[384,1792]{1,0:T(8,128)(2,1)S(1)} %get-tuple-element.92), channel_id=1, source_target_pairs={{0,8},{8,0},{16,24},{24,16},{1,9},{9,1},{17,25},{25,17},{2,10},{10... | collective-permute-start | bytes 4128776 | tf_op jit(solution)/shard_map/ppermute | solution.py:71
  345.6 33.1 %collective-permute-start.42 = (bf16[384,1792]{1,0:T(8,128)(2,1)S(1)}, bf16[384,1792]{1,0:T(8,128)(2,1)S(1)}, u32[]{:S(2)}, u32[]{:S(2)}) collective-permute-start(bf16[384,1792]{1,0:T(8,128)(2,1)S(1)} %get-tuple-element.94), channel_id=1, source_target_pairs={{0,16},{8,24},{16,0},{24,8},{1,17},{9,25},{17,1},{25,9},{2,18},{10... | collective-permute-start | bytes 4128776 | tf_op jit(solution)/shard_map/ppermute | solution.py:71
  347.2 41.6 %collective-permute-start.30 = (bf16[384,640]{1,0:T(8,128)(2,1)S(1)}, bf16[384,640]{1,0:T(8,128)(2,1)S(1)}, u32[]{:S(2)}, u32[]{:S(2)}) collective-permute-start(bf16[384,640]{1,0:T(8,128)(2,1)S(1)} %get-tuple-element.76), channel_id=1, source_target_pairs={{0,8},{8,0},{16,24},{24,16},{1,9},{9,1},{17,25},{25,17},{2,10},{10... | collective-permute-start | bytes 1474568 | tf_op jit(solution)/shard_map/ppermute | solution.py:71
  348.7 40.5 %collective-permute-start.31 = (bf16[384,640]{1,0:T(8,128)(2,1)S(1)}, bf16[384,640]{1,0:T(8,128)(2,1)S(1)}, u32[]{:S(2)}, u32[]{:S(2)}) collective-permute-start(bf16[384,640]{1,0:T(8,128)(2,1)S(1)} %get-tuple-element.78), channel_id=1, source_target_pairs={{0,16},{8,24},{16,0},{24,8},{1,17},{9,25},{17,1},{25,9},{2,18},{10... | collective-permute-start | bytes 1474568 | tf_op jit(solution)/shard_map/ppermute | solution.py:71
  379.9 35.6 %collective-permute-start.43 = (bf16[192,1792]{1,0:T(8,128)(2,1)S(1)}, bf16[192,1792]{1,0:T(8,128)(2,1)S(1)}, u32[]{:S(2)}, u32[]{:S(2)}) collective-permute-start(bf16[192,1792]{1,0:T(8,128)(2,1)S(1)} %get-tuple-element.96), channel_id=1, source_target_pairs={{0,16},{8,24},{16,0},{24,8},{1,17},{9,25},{17,1},{25,9},{2,18},{10... | collective-permute-start | bytes 2064392 | tf_op jit(solution)/shard_map/ppermute | solution.py:71
  380.4 35.1 %collective-permute-start.44 = (bf16[192,1792]{1,0:T(8,128)(2,1)S(1)}, bf16[192,1792]{1,0:T(8,128)(2,1)S(1)}, u32[]{:S(2)}, u32[]{:S(2)}) collective-permute-start(bf16[192,1792]{1,0:T(8,128)(2,1)S(1)} %get-tuple-element.98), channel_id=1, source_target_pairs={{0,8},{8,0},{16,24},{24,16},{1,9},{9,1},{17,25},{25,17},{2,10},{10... | collective-permute-start | bytes 2064392 | tf_op jit(solution)/shard_map/ppermute | solution.py:71
  390.1 18.0 %collective-permute-start.32 = (bf16[192,640]{1,0:T(8,128)(2,1)S(1)}, bf16[192,640]{1,0:T(8,128)(2,1)S(1)}, u32[]{:S(2)}, u32[]{:S(2)}) collective-permute-start(bf16[192,640]{1,0:T(8,128)(2,1)S(1)} %get-tuple-element.80), channel_id=1, source_target_pairs={{0,16},{8,24},{16,0},{24,8},{1,17},{9,25},{17,1},{25,9},{2,18},{10... | collective-permute-start | bytes 737288 | tf_op jit(solution)/shard_map/ppermute | solution.py:71
  390.6 17.6 %collective-permute-start.33 = (bf16[192,640]{1,0:T(8,128)(2,1)S(1)}, bf16[192,640]{1,0:T(8,128)(2,1)S(1)}, u32[]{:S(2)}, u32[]{:S(2)}) collective-permute-start(bf16[192,640]{1,0:T(8,128)(2,1)S(1)} %get-tuple-element.82), channel_id=1, source_target_pairs={{0,8},{8,0},{16,24},{24,16},{1,9},{9,1},{17,25},{25,17},{2,10},{10... | collective-permute-start | bytes 737288 | tf_op jit(solution)/shard_map/ppermute | solution.py:71
  408.8 13.5 %collective-permute-start.34 = (bf16[48,1280]{1,0:T(8,128)(2,1)S(1)}, bf16[48,1280]{1,0:T(8,128)(2,1)S(1)}, u32[]{:S(2)}, u32[]{:S(2)}) collective-permute-start(bf16[48,1280]{1,0:T(8,128)(2,1)S(1)} %get-tuple-element.84), channel_id=1, source_target_pairs={{0,2},{1,3},{2,4},{3,5},{4,6},{5,7},{6,0},{7,1},{8,10},{9,11},{10,... | collective-permute-start | bytes 368648 | tf_op jit(solution)/shard_map/ppermute | solution.py:67
  416.4 40.2 %collective-permute-start.45 = (bf16[48,3584]{1,0:T(8,128)(2,1)S(1)}, bf16[48,3584]{1,0:T(8,128)(2,1)S(1)}, u32[]{:S(2)}, u32[]{:S(2)}) collective-permute-start(bf16[48,3584]{1,0:T(8,128)(2,1)S(1)} %get-tuple-element.100), channel_id=1, source_target_pairs={{0,2},{1,3},{2,4},{3,5},{4,6},{5,7},{6,0},{7,1},{8,10},{9,11},{10,... | collective-permute-start | bytes 1032200 | tf_op jit(solution)/shard_map/ppermute | solution.py:67
  416.5 42.4 %collective-permute-start.46 = (bf16[48,3584]{1,0:T(8,128)(2,1)S(1)}, bf16[48,3584]{1,0:T(8,128)(2,1)S(1)}, u32[]{:S(2)}, u32[]{:S(2)}) collective-permute-start(bf16[48,3584]{1,0:T(8,128)(2,1)S(1)} %get-tuple-element.101), channel_id=1, source_target_pairs={{0,4},{1,5},{2,6},{3,7},{4,0},{5,1},{6,2},{7,3},{8,12},{9,13},{10,... | collective-permute-start | bytes 1032200 | tf_op jit(solution)/shard_map/ppermute | solution.py:67
  416.6 42.4 %collective-permute-start.47 = (bf16[48,3584]{1,0:T(8,128)(2,1)S(1)}, bf16[48,3584]{1,0:T(8,128)(2,1)S(1)}, u32[]{:S(2)}, u32[]{:S(2)}) collective-permute-start(bf16[48,3584]{1,0:T(8,128)(2,1)S(1)} %get-tuple-element.102), channel_id=1, source_target_pairs={{0,6},{1,7},{2,0},{3,1},{4,2},{5,3},{6,4},{7,5},{8,14},{9,15},{10,... | collective-permute-start | bytes 1032200 | tf_op jit(solution)/shard_map/ppermute | solution.py:67
  420.3 34.5 %collective-permute-start.35 = (bf16[48,1280]{1,0:T(8,128)(2,1)S(1)}, bf16[48,1280]{1,0:T(8,128)(2,1)S(1)}, u32[]{:S(2)}, u32[]{:S(2)}) collective-permute-start(bf16[48,1280]{1,0:T(8,128)(2,1)S(1)} %get-tuple-element.85), channel_id=1, source_target_pairs={{0,4},{1,5},{2,6},{3,7},{4,0},{5,1},{6,2},{7,3},{8,12},{9,13},{10,... | collective-permute-start | bytes 368648 | tf_op jit(solution)/shard_map/ppermute | solution.py:67
  422.3 32.4 %collective-permute-start.36 = (bf16[48,1280]{1,0:T(8,128)(2,1)S(1)}, bf16[48,1280]{1,0:T(8,128)(2,1)S(1)}, u32[]{:S(2)}, u32[]{:S(2)}) collective-permute-start(bf16[48,1280]{1,0:T(8,128)(2,1)S(1)} %get-tuple-element.86), channel_id=1, source_target_pairs={{0,6},{1,7},{2,0},{3,1},{4,2},{5,3},{6,4},{7,5},{8,14},{9,15},{10,... | collective-permute-start | bytes 368648 | tf_op jit(solution)/shard_map/ppermute | solution.py:67
  456.0 22.6 %collective-permute-start.38 = (bf16[48,1280]{1,0:T(8,128)(2,1)S(1)}, bf16[48,1280]{1,0:T(8,128)(2,1)S(1)}, u32[]{:S(2)}, u32[]{:S(2)}) collective-permute-start(bf16[48,1280]{1,0:T(8,128)(2,1)S(1)} %shard_map.289.own), channel_id=1, source_target_pairs={{0,16},{8,24},{16,0},{24,8},{1,17},{9,25},{17,1},{25,9},{2,18},{10... | collective-permute-start | bytes 368648 | tf_op jit(solution)/shard_map/ppermute | solution.py:71
  456.7 22.0 %collective-permute-start.39 = (bf16[48,1280]{1,0:T(8,128)(2,1)S(1)}, bf16[48,1280]{1,0:T(8,128)(2,1)S(1)}, u32[]{:S(2)}, u32[]{:S(2)}) collective-permute-start(bf16[48,1280]{1,0:T(8,128)(2,1)S(1)} %shard_map.289.own), channel_id=1, source_target_pairs={{0,24},{8,16},{16,8},{24,0},{1,25},{9,17},{17,9},{25,1},{2,26},{10... | collective-permute-start | bytes 368648 | tf_op jit(solution)/shard_map/ppermute | solution.py:71
  459.6 21.1 %collective-permute-start.48 = (bf16[48,3584]{1,0:T(8,128)(2,1)S(1)}, bf16[48,3584]{1,0:T(8,128)(2,1)S(1)}, u32[]{:S(2)}, u32[]{:S(2)}) collective-permute-start(bf16[48,3584]{1,0:T(8,128)(2,1)S(1)} %shard_map.294.own), channel_id=1, source_target_pairs={{0,8},{8,0},{16,24},{24,16},{1,9},{9,1},{17,25},{25,17},{2,10},{10... | collective-permute-start | bytes 1032200 | tf_op jit(solution)/shard_map/ppermute | solution.py:71
  460.3 20.4 %collective-permute-start.49 = (bf16[48,3584]{1,0:T(8,128)(2,1)S(1)}, bf16[48,3584]{1,0:T(8,128)(2,1)S(1)}, u32[]{:S(2)}, u32[]{:S(2)}) collective-permute-start(bf16[48,3584]{1,0:T(8,128)(2,1)S(1)} %shard_map.294.own), channel_id=1, source_target_pairs={{0,16},{8,24},{16,0},{24,8},{1,17},{9,25},{17,1},{25,9},{2,18},{10... | collective-permute-start | bytes 1032200 | tf_op jit(solution)/shard_map/ppermute | solution.py:71
  461.1 19.7 %collective-permute-start.50 = (bf16[48,3584]{1,0:T(8,128)(2,1)S(1)}, bf16[48,3584]{1,0:T(8,128)(2,1)S(1)}, u32[]{:S(2)}, u32[]{:S(2)}) collective-permute-start(bf16[48,3584]{1,0:T(8,128)(2,1)S(1)} %shard_map.294.own), channel_id=1, source_target_pairs={{0,24},{8,16},{16,8},{24,0},{1,25},{9,17},{17,9},{25,1},{2,26},{10... | collective-permute-start | bytes 1032200 | tf_op jit(solution)/shard_map/ppermute | solution.py:71
  (24 other events, 564.3 us)
